TPU v7x, 256 devices: a whole 4x4x8 slice. The times are simulated.
256 devices in a mesh: expert: 16 (over x, y_lo, core), tensor: 2 (over y_hi), replica: 8 (over z).
Axes of the slice: x: 4, y: 4 (y_hi: 2, y_lo: 2; y = y_hi * 2 + y_lo), z: 8, core: 2. Of those that a mesh axis runs over, the one named last changes fastest.
Arguments:
- tokens: bfloat16 [2048, 3072], P('expert', 'replica'), may hold values from -6 to 6
- cotangent: bfloat16 [2048, 3072], P('expert', 'replica'), may hold values from -4 to 4
- gate_values: float32 [2048, 4], P('expert'), may hold values from 0.05 to 1
- expert_ids: int32 [2048, 4], P('expert'), may hold values from 0 to 15, all different within a row; in each aligned block of 128 rows (0 to 127, 128 to 255, ...) at most 48 rows name the same one
- gate_weight: bfloat16 [16, 3072, 5376], P('expert', 'replica', 'tensor'), may hold values from -0.109375 to 0.109375
- up_weight: bfloat16 [16, 3072, 5376], P('expert', 'replica', 'tensor'), may hold values from -0.109375 to 0.109375
- down_weight: bfloat16 [16, 5376, 3072], P('expert', 'tensor', 'replica'), may hold values from -0.078125 to 0.078125
- block_ids: int32 [16, 2], P('expert'), may hold values from 0 to 23, as said below
- feedback: bfloat16 [16, 3072, 5376], P('expert', 'replica', 'tensor'), may hold values from -6 to 6
Outputs:
- token_grad: bfloat16 [2048, 3072], P(('expert', 'tensor'), 'replica')
- block_sums: float32 [16, 2, 128, 5376], P('expert', None, None, 'tensor')
- new_feedback: bfloat16 [16, 3072, 5376], P('expert', 'replica', 'tensor')
Inputs may be any that keep to these rules, and one draw needn't show every extreme that they name: `expert_ids`: in the rows of one token group no expert is named more than 48 times, and each row names 4 different experts. `block_ids`: for each expert the 2 block numbers are different.
All inputs are finite; a program needn't handle non-finite values.
Results may differ from a plain program's by a relative error of at most 0.03.
Values may be sent and summed in bfloat16 or wider, within the bound.
No kernel may reach another device: no remote copies, remote signals or barrier semaphores. Data moves between devices by JAX's collectives and lax.ppermute only.
A program may use at most 128 MiB of HBM per device.

v0:
```python
import jax
import jax.numpy as jnp
from jax import lax
from jax.sharding import PartitionSpec as P

BLOCK = 128


def routing_tables(expert_ids, gate_values, experts, capacity):
    tok_rows, top_count = expert_ids.shape
    flat_ids = expert_ids.reshape(-1)
    choose = (flat_ids[:, None] == jnp.arange(experts, dtype=jnp.int32)[None, :]).astype(jnp.int32)
    before = jnp.cumsum(choose, axis=0) - choose
    slot_index = jnp.sum(before * choose, axis=1)
    target = (flat_ids * capacity + slot_index).reshape(tok_rows, top_count)
    matches = target[None, :, :] == jnp.arange(experts * capacity, dtype=jnp.int32)[:, None, None]
    placing = jnp.any(matches, axis=2).astype(jnp.bfloat16)
    slot_gate = jnp.sum(jnp.where(matches, gate_values[None, :, :], jnp.float32(0.0)), axis=(1, 2))
    return (placing, slot_gate)


def backward_gates(gate_pre, up_pre, hidden_grad):
    squashed = jax.nn.sigmoid(gate_pre)
    grad_gate = (hidden_grad * up_pre * squashed * (1.0 + gate_pre * (1.0 - squashed))).astype(
        jnp.bfloat16
    )
    grad_up = (hidden_grad * gate_pre * squashed).astype(jnp.bfloat16)
    return (grad_gate, grad_up)


def body(
    tokens,
    cotangent,
    gate_values,
    expert_ids,
    gate_weight,
    up_weight,
    down_weight,
    block_ids,
    feedback,
):
    groups = lax.axis_size("expert")
    experts = groups * gate_weight.shape[0]
    tok_rows, top_count = expert_ids.shape
    capacity = min(tok_rows, tok_rows * top_count * 3 // (2 * experts))
    features = tokens.shape[1]
    placing, slot_gate = routing_tables(expert_ids, gate_values, experts, capacity)
    sent_rows = jnp.dot(placing, tokens, preferred_element_type=jnp.float32).astype(jnp.bfloat16)
    sent_rows = sent_rows.reshape(experts, capacity, features)
    sent_grads = (
        jnp.dot(placing, cotangent, preferred_element_type=jnp.float32) * slot_gate[:, None]
    ).astype(jnp.bfloat16)
    sent_grads = sent_grads.reshape(experts, capacity, features)
    w_gate = gate_weight[0]
    w_up = up_weight[0]
    w_down = down_weight[0]
    arrived, arrived_grads = (
        lax.all_to_all(sent_rows, "expert", split_axis=0, concat_axis=0, tiled=True),
        lax.all_to_all(sent_grads, "expert", split_axis=0, concat_axis=0, tiled=True),
    )
    slot_rows = arrived.reshape(-1, features)
    gate_part = jnp.dot(slot_rows, w_gate, preferred_element_type=jnp.float32)
    up_part = jnp.dot(slot_rows, w_up, preferred_element_type=jnp.float32)
    grad_rows = arrived_grads.reshape(-1, features)
    hidden_part = jnp.einsum("sd,fd->sf", grad_rows, w_down, preferred_element_type=jnp.float32)
    gate_pre, up_pre, hidden_grad = (
        lax.psum_scatter(
            gate_part.astype(jnp.bfloat16), "replica", scatter_dimension=0, tiled=True
        ).astype(jnp.float32),
        lax.psum_scatter(
            up_part.astype(jnp.bfloat16), "replica", scatter_dimension=0, tiled=True
        ).astype(jnp.float32),
        lax.psum_scatter(
            hidden_part.astype(jnp.bfloat16), "replica", scatter_dimension=0, tiled=True
        ).astype(jnp.float32),
    )
    grad_gate, grad_up = backward_gates(gate_pre, up_pre, hidden_grad)
    grad_gate, grad_up = (
        lax.all_gather(grad_gate, "replica", axis=0, tiled=True),
        lax.all_gather(grad_up, "replica", axis=0, tiled=True),
    )
    gradient = jnp.einsum(
        "sd,sf->df", slot_rows, grad_gate, preferred_element_type=jnp.float32
    ) + feedback[0].astype(jnp.float32)
    local_blocks = gradient.shape[0] // BLOCK
    local_ids = block_ids[0] - lax.axis_index("replica") * local_blocks
    holding = jnp.logical_and(local_ids >= 0, local_ids < local_blocks)
    blocked = gradient.reshape(local_blocks, BLOCK, gradient.shape[1])
    picked = jnp.take(blocked, jnp.clip(local_ids, 0, local_blocks - 1), axis=0)
    picked = jnp.where(holding[:, None, None], picked, jnp.float32(0.0))
    struck = jnp.any(
        local_ids[:, None] == jnp.arange(local_blocks, dtype=jnp.int32)[None, :], axis=0
    )
    retained = (
        jnp.where(struck[:, None, None], jnp.float32(0.0), blocked)
        .reshape(gradient.shape)
        .astype(jnp.bfloat16)
    )
    block_sums = lax.psum(picked.astype(jnp.bfloat16), "replica").astype(jnp.float32)
    partial_grad = jnp.einsum("sf,df->sd", grad_gate, w_gate, preferred_element_type=jnp.float32)
    partial_grad = (
        partial_grad + jnp.einsum("sf,df->sd", grad_up, w_up, preferred_element_type=jnp.float32)
    ).astype(jnp.bfloat16)
    partial_grad = partial_grad.reshape(experts, capacity, features)
    returned = lax.all_to_all(partial_grad, "expert", split_axis=0, concat_axis=0, tiled=True)
    combined = jnp.dot(
        placing.T,
        returned.reshape(experts * capacity, features),
        preferred_element_type=jnp.float32,
    )
    token_grad = lax.psum_scatter(
        combined.astype(jnp.bfloat16), "tensor", scatter_dimension=0, tiled=True
    )
    return (token_grad, block_sums[None], retained[None])


def solution(mesh):
    return jax.shard_map(
        body,
        mesh=mesh,
        in_specs=(
            P("expert", "replica"),
            P("expert", "replica"),
            P("expert", None),
            P("expert", None),
            P("expert", "replica", "tensor"),
            P("expert", "replica", "tensor"),
            P("expert", "tensor", "replica"),
            P("expert", None),
            P("expert", "replica", "tensor"),
        ),
        out_specs=(
            P(("expert", "tensor"), "replica"),
            P("expert", None, None, "tensor"),
            P("expert", "replica", "tensor"),
        ),
        check_vma=False,
    )
```

profile of v0, /device:TPU:8, one launch (start us, length us, event | category | flops | bytes accessed | tf_op | source)
XLA Modules:
  0.0 416.4 jit_solution(15116542466653855632)
XLA Ops:
  7.2 0.0 reduce-scatter.5.cloned.1.call-start
  7.2 0.9 copy.26
  8.2 0.1 eq.55
  8.3 0.1 eq.51
  8.4 1.2 reduce-window.6
  9.5 0.2 slice_reduce_fusion
  9.8 0.1 fusion.28
  9.9 0.1 reduce_sum.21
  10.0 0.1 copy.29
  10.1 0.9 multiply_add_fusion
  10.9 0.2 fusion.8
  11.1 0.9 select_reduce_fusion
  12.1 1.2 fusion.16
  13.3 15.9 %all_to_all.15 = bf16[16,48,384]{2,1,0:T(8,128)(2,1)S(1)} all-to-all(bf16[16,48,384]{2,1,0:T(8,128)(2,1)S(1)} %bitcast.77), channel_id=1, replica_groups=mesh['expert'=16,'tensor'=2,'replica'=8] {'expert'}, dimensions={0} | all-to-all | bytes 1179648 | tf_op jit(solution)/shard_map/all_to_all | solution.py:59
  29.2 4.3 %convolution_convert_fusion.2 = bf16[768,2688]{1,0:T(8,128)(2,1)} fusion(bf16[768,384]{1,0:T(8,128)(2,1)S(1)} %bitcast.79, bf16[1,2688,384]{2,1,0:T(8,128)(2,1)S(1)} %copy-done.3), kind=kOutput, calls=%fused_computation.3 | convolution fusion | flops 1587511296 | bytes 6782976 | tf_op jit(solution)/shard_map/sd,fd->sf/dot_general | solution.py:65
  33.5 0.0 reduce-scatter.5.cloned.1.call-update
  33.5 0.0 reduce-scatter.7.cloned.1.call-start
  33.5 0.8 copy-done.1
  34.4 0.3 convolution_convert_fusion.3
  34.7 14.2 %all_to_all.16 = bf16[16,48,384]{2,1,0:T(8,128)(2,1)S(1)} all-to-all(bf16[16,48,384]{2,1,0:T(8,128)(2,1)S(1)} %bitcast.78), channel_id=1, replica_groups=mesh['expert'=16,'tensor'=2,'replica'=8] {'expert'}, dimensions={0} | all-to-all | bytes 1179648 | tf_op jit(solution)/shard_map/all_to_all | solution.py:58
  48.8 5.9 %convolution_convert_fusion.1 = bf16[768,2688]{1,0:T(8,128)(2,1)} fusion(bf16[768,384]{1,0:T(8,128)(2,1)S(1)} %bitcast.73, bf16[1,384,2688]{2,1,0:T(8,128)(2,1)} %param.14), kind=kOutput, calls=%fused_computation.2 | convolution fusion | flops 1587511296 | bytes 6782976 | tf_op jit(solution)/shard_map/dot_general | solution.py:63
  54.7 0.0 reduce-scatter.9.cloned.1.call-start
  54.8 4.3 %convolution_convert_fusion = bf16[768,2688]{1,0:T(8,128)(2,1)} fusion(bf16[768,384]{1,0:T(8,128)(2,1)S(1)} %bitcast.74, bf16[1,384,2688]{2,1,0:T(8,128)(2,1)S(1)} %copy-done), kind=kOutput, calls=%fused_computation.1 | convolution fusion | flops 1587511296 | bytes 6782976 | tf_op jit(solution)/shard_map/dot_general | solution.py:62
  59.1 0.0 all-gather.3.cloned.1.call-start
  59.2 30.8 %reduce-scatter.5.cloned.1.call-done = bf16[96,2688]{1,0:T(8,128)(2,1)} async-done(((bf16[768,2688]{1,0:T(8,128)(2,1)}), bf16[96,2688]{1,0:T(8,128)(2,1)}) %reduce-scatter.5.cloned.1.call-update) | async-done | bytes 516112 | tf_op jit(solution)/shard_map/reduce_scatter | solution.py:73
  90.0 56.1 %reduce-scatter.7.cloned.1.call-done = bf16[96,2688]{1,0:T(8,128)(2,1)} async-done(((bf16[768,2688]{1,0:T(8,128)(2,1)}), bf16[96,2688]{1,0:T(8,128)(2,1)}) %reduce-scatter.7.cloned.1.call-update) | async-done | bytes 516112 | tf_op jit(solution)/shard_map/reduce_scatter | solution.py:70
  146.1 55.9 %reduce-scatter.9.cloned.1.call-done = bf16[96,2688]{1,0:T(8,128)(2,1)} async-done(((bf16[768,2688]{1,0:T(8,128)(2,1)}), bf16[96,2688]{1,0:T(8,128)(2,1)}) %reduce-scatter.9.cloned.1.call-update) | async-done | bytes 516112 | tf_op jit(solution)/shard_map/reduce_scatter | solution.py:67
  202.1 2.8 fusion.25
  204.9 0.0 all-gather.5.cloned.1.call-start
  205.0 0.5 all-gather.5.cloned.1.call-update
  205.5 0.2 all-reduce.2.cloned.1.call-start
  205.8 52.1 %all-gather.3.cloned.1.call-done = bf16[768,2688]{1,0:T(8,128)(2,1)} async-done(((bf16[96,2688]{1,0:T(8,128)(2,1)}), bf16[768,2688]{1,0:T(8,128)(2,1)}) %all-gather.3.cloned.1.call-update) | async-done | bytes 4128784 | tf_op jit(solution)/shard_map/all_gather | solution.py:79
  257.9 6.0 %convolution_add_fusion = bf16[384,2688]{1,0:T(8,128)(2,1)} fusion(bf16[768,384]{1,0:T(8,128)(2,1)S(1)} %bitcast.75, bf16[768,2688]{1,0:T(8,128)(2,1)} %all-gather.3.cloned.1.call-done, bf16[1,384,2688]{2,1,0:T(8,128)(2,1)} %param.17), kind=kOutput, calls=%fused_computation.4 | convolution fusion | flops 1588543488 | bytes 8847360 | tf_op jit(solution)/shard_map/sd,sf->df/dot_general | solution.py:82
  264.0 2.3 gather_fusion
  266.3 1.5 fusion.9
  267.8 4.6 %fusion.1 = f32[768,384]{1,0:T(8,128)S(1)} fusion(bf16[768,2688]{1,0:T(8,128)(2,1)} %all-gather.3.cloned.1.call-done, bf16[1,384,2688]{2,1,0:T(8,128)(2,1)S(1)} %copy-done), kind=kOutput, calls=%fused_computation.8 | convolution fusion | flops 1585446912 | bytes 7372800 | tf_op jit(solution)/shard_map/sf,df->sd/dot_general | solution.py:100
  272.3 40.2 %all-gather.5.cloned.1.call-done = bf16[768,2688]{1,0:T(8,128)(2,1)} async-done(((bf16[96,2688]{1,0:T(8,128)(2,1)}), bf16[768,2688]{1,0:T(8,128)(2,1)}) %all-gather.5.cloned.1.call-update) | async-done | bytes 4128784 | tf_op jit(solution)/shard_map/all_gather | solution.py:80
  312.5 6.0 %fusion.13 = bf16[768,384]{1,0:T(8,128)(2,1)} fusion(f32[768,384]{1,0:T(8,128)S(1)} %fusion.1, bf16[768,2688]{1,0:T(8,128)(2,1)} %all-gather.5.cloned.1.call-done, bf16[1,384,2688]{2,1,0:T(8,128)(2,1)} %param.14), kind=kOutput, calls=%fused_computation.25 | convolution fusion | flops 1586036736 | bytes 7962624 | tf_op jit(solution)/shard_map/sf,df->sd/dot_general | solution.py:102
  318.5 5.7 %all-to-all-start.2 = ((bf16[16,48,384]{2,1,0:T(8,128)(2,1)}), bf16[16,48,384]{2,1,0:T(8,128)(2,1)S(1)}, u32[]{:S(2)}, u32[]{:S(2)}) async-start(bf16[16,48,384]{2,1,0:T(8,128)(2,1)} %bitcast.8), calls=%async_computation.5 | async-start | bytes 1179648 | tf_op jit(solution)/shard_map/all_to_all | solution.py:105
  324.2 0.0 reduce-scatter.11.cloned.1.call-start
  324.3 0.1 compare_reduce_fusion
  324.4 0.1 broadcast_bitcast_fusion
  324.5 9.8 %all-to-all-done.2 = bf16[16,48,384]{2,1,0:T(8,128)(2,1)S(1)} async-done(((bf16[16,48,384]{2,1,0:T(8,128)(2,1)}), bf16[16,48,384]{2,1,0:T(8,128)(2,1)S(1)}, u32[]{:S(2)}, u32[]{:S(2)}) %all-to-all-start.2) | async-done | bytes 589856 | tf_op jit(solution)/shard_map/all_to_all | solution.py:105
  334.3 0.9 convolution_convert_fusion.4
  335.2 3.3 fusion
  338.5 53.2 %all-reduce.2.cloned.1.call-done = bf16[1,2,128,2688]{3,2,1,0:T(8,128)(2,1)} async-done(((bf16[1,2,128,2688]{3,2,1,0:T(8,128)(2,1)}), bf16[1,2,128,2688]{3,2,1,0:T(8,128)(2,1)}) %all-reduce.2.cloned.1.call-update) | async-done | bytes 1376272 | tf_op jit(solution)/shard_map/psum | solution.py:99
  391.7 3.1 broadcast_in_dim.74
  394.8 14.8 %reduce-scatter.11.cloned.1.call-done = bf16[64,384]{1,0:T(8,128)(2,1)} async-done(((bf16[128,384]{1,0:T(8,128)(2,1)}), bf16[64,384]{1,0:T(8,128)(2,1)}) %reduce-scatter.11.cloned.1.call-update) | async-done | bytes 49168 | tf_op jit(solution)/shard_map/reduce_scatter | solution.py:111
  (19 shorter events, 0.2 us)
Async XLA Ops:
  7.2 47.6 %copy-start = (bf16[1,384,2688]{2,1,0:T(8,128)(2,1)S(1)}, bf16[1,384,2688]{2,1,0:T(8,128)(2,1)}, u32[]{:S(2)}) copy-start(bf16[1,384,2688]{2,1,0:T(8,128)(2,1)} %param.13) | copy-start | bytes 6193156
  7.2 82.9 %reduce-scatter.5.cloned.1.call-start = ((), (), s32[]{:S(2)}) async-start(), calls=%async_computation.7 | async-start | bytes 4644864 | tf_op jit(solution)/shard_map/reduce_scatter | solution.py:73
  10.1 19.1 %copy-start.3 = (bf16[1,2688,384]{2,1,0:T(8,128)(2,1)S(1)}, bf16[1,2688,384]{2,1,0:T(8,128)(2,1)}, u32[]{:S(2)}) copy-start(bf16[1,2688,384]{2,1,0:T(8,128)(2,1)} %param.15) | copy-start | bytes 6193156
  33.5 0.9 copy-start.1
  33.5 112.6 %reduce-scatter.7.cloned.1.call-start = ((), (), s32[]{:S(2)}) async-start(), calls=%async_computation.8 | async-start | bytes 4644864 | tf_op jit(solution)/shard_map/reduce_scatter | solution.py:70
  54.7 147.3 %reduce-scatter.9.cloned.1.call-start = ((), (), s32[]{:S(2)}) async-start(), calls=%async_computation.9 | async-start | bytes 4644864 | tf_op jit(solution)/shard_map/reduce_scatter | solution.py:67
  59.1 146.6 %copy-start.2 = (s32[1,2]{1,0:T(1,128)S(1)}, s32[1,2]{1,0:T(1,128)}, u32[]{:S(2)}) copy-start(s32[1,2]{1,0:T(1,128)} %param.16) | copy-start | bytes 28
  59.1 198.8 %all-gather.3.cloned.1.call-start = ((), (), s32[]{:S(2)}) async-start(), calls=%async_computation.10 | async-start | bytes 4644864 | tf_op jit(solution)/shard_map/all_gather | solution.py:79
  204.9 107.6 %all-gather.5.cloned.1.call-start = ((), (), s32[]{:S(2)}) async-start(), calls=%async_computation.11 | async-start | bytes 4644864 | tf_op jit(solution)/shard_map/all_gather | solution.py:80
  205.5 186.2 %all-reduce.2.cloned.1.call-start = ((), (), s32[]{:S(2)}) async-start(), calls=%async_computation.13 | async-start | bytes 2752512 | tf_op jit(solution)/shard_map/psum | solution.py:99
  318.5 15.7 %all-to-all-start.2 = ((bf16[16,48,384]{2,1,0:T(8,128)(2,1)}), bf16[16,48,384]{2,1,0:T(8,128)(2,1)S(1)}, u32[]{:S(2)}, u32[]{:S(2)}) async-start(bf16[16,48,384]{2,1,0:T(8,128)(2,1)} %bitcast.8), calls=%async_computation.5 | async-start | bytes 1179648 | tf_op jit(solution)/shard_map/all_to_all | solution.py:105
  324.2 85.3 %reduce-scatter.11.cloned.1.call-start = ((), (), s32[]{:S(2)}) async-start(), calls=%async_computation.12 | async-start | bytes 147456 | tf_op jit(solution)/shard_map/reduce_scatter | solution.py:111
Sparse Core Ops, SparseCore 0:
  33.6 56.3 reduce-scatter.4
  92.8 53.2 reduce-scatter.6
  148.7 53.2 reduce-scatter.8
  205.0 52.8 all-gather.2
  259.7 52.7 all-gather.4
  315.4 76.2 all-reduce.1
  394.8 14.7 reduce-scatter.10
where the time goes:
time: 419 us; the launch traced here: 416 us
  waiting for transfers between devices  314 us (75%)
  matrix products  33.6 us (8%)
  blocking collectives  30 us (7%)
  between operations  14.3 us (3%)
  other arithmetic  14 us (3%)
  starting transfers between devices  6.19 us (1%)
  local copies, waits for them, and re-layouts  4.76 us (1%)
    reduce_scatter x1, waiting for transfers between devices, body(): lax.psum_scatter(up_part.astype(jnp.bfloat16), 'replica', scatter_dimensi...  56.1 us
    reduce_scatter x1, waiting for transfers between devices, body(): lax.psum_scatter(gate_part.astype(jnp.bfloat16), 'replica', scatter_dimen...  55.9 us
    psum x1, waiting for transfers between devices, body(): lax.psum(picked.astype(jnp.bfloat16), 'replica').astype(jnp.float32)  53.2 us
    all_gather x1, waiting for transfers between devices, body(): lax.all_gather(grad_gate, 'replica', axis=0, tiled=True)  52.1 us
    all_gather x1, waiting for transfers between devices, body(): lax.all_gather(grad_up, 'replica', axis=0, tiled=True)  40.2 us
    reduce_scatter x1, waiting for transfers between devices, body(): lax.psum_scatter(hidden_part.astype(jnp.bfloat16), 'replica', scatter_dim...  30.8 us
    all_to_all x1, blocking collectives, body(): lax.all_to_all(sent_grads, 'expert', split_axis=0, concat_axis=0, tiled=T...  15.9 us
    reduce_scatter x1, waiting for transfers between devices, body(): lax.psum_scatter(combined.astype(jnp.bfloat16), 'tensor', scatter_dimensi...  14.8 us
  transfers between devices with their start and end apart: 8, of which 8 were waited for; matrix products, arithmetic and copies ran while one was open for 9% of the time, Pallas kernels for 0%

commit v1 on v0

v1 whole, which is shorter than its diff:
```python
import jax
import jax.numpy as jnp
from jax import lax
from jax.experimental import pallas as pl
from jax.experimental.pallas import tpu as pltpu
from jax.sharding import PartitionSpec as P

BLOCK = 128


def routing_tables(expert_ids, gate_values, experts, capacity):
    tok_rows, top_count = expert_ids.shape
    flat_ids = expert_ids.reshape(-1)
    choose = (flat_ids[:, None] == jnp.arange(experts, dtype=jnp.int32)[None, :]).astype(jnp.int32)
    before = jnp.cumsum(choose, axis=0) - choose
    slot_index = jnp.sum(before * choose, axis=1)
    target = (flat_ids * capacity + slot_index).reshape(tok_rows, top_count)
    matches = target[None, :, :] == jnp.arange(experts * capacity, dtype=jnp.int32)[:, None, None]
    placing = jnp.any(matches, axis=2).astype(jnp.bfloat16)
    slot_gate = jnp.sum(jnp.where(matches, gate_values[None, :, :], jnp.float32(0.0)), axis=(1, 2))
    return (placing, slot_gate)


MIB = 1024 * 1024
SPARE = 48


def shift_by(distance, size):
    return [(i, (i + distance) % size) for i in range(size)]


def split_kernel(own_hidden, here_ref, gate_ref, up_ref, *refs):
    outs, turned = refs[:-1], refs[-1]
    columns = gate_ref.shape[1]

    @pl.loop(0, columns // BLOCK)
    def _(tile):
        at = pl.ds(pl.multiple_of(tile * BLOCK, BLOCK), BLOCK)
        turned[0, at, :] = gate_ref[:, at].T
        turned[1, at, :] = up_ref[:, at].T

    for d, out in enumerate(outs):
        owner = lax.rem(here_ref[0] + d, len(outs))
        rows = pl.ds(pl.multiple_of(owner * own_hidden, 16), own_hidden)
        out[:own_hidden, :] = turned[0, rows, :]
        out[own_hidden:, :] = turned[1, rows, :]


def split_weights(w_gate, w_up, here, shares):
    features, hidden = w_gate.shape
    own_hidden = hidden // shares
    piece = jax.ShapeDtypeStruct((2 * own_hidden, features), jnp.bfloat16)
    return pl.pallas_call(
        lambda *refs: split_kernel(own_hidden, *refs),
        in_specs=[
            pl.BlockSpec(memory_space=pltpu.SMEM),
            pl.BlockSpec(memory_space=pltpu.VMEM),
            pl.BlockSpec(memory_space=pltpu.VMEM),
        ],
        out_specs=[pl.BlockSpec(memory_space=pltpu.VMEM)] * shares,
        out_shape=[piece] * shares,
        scratch_shapes=[pltpu.VMEM((2, hidden, features), jnp.bfloat16)],
        cost_estimate=pl.CostEstimate(
            flops=0, bytes_accessed=8 * hidden * features, transcendentals=0
        ),
        compiler_params=pltpu.CompilerParams(vmem_limit_bytes=58 * MIB),
    )(here.reshape(1), w_gate, w_up)


def pick_kernel(at_ref, holds_ref, stored_ref, out_ref):
    wide, select = out_ref.shape[1], at_ref.shape[0]
    whole = stored_ref.shape[1] // wide
    rest = stored_ref.shape[1] - whole * wide
    for i in range(select):
        rows = stored_ref[pl.ds(pl.multiple_of(at_ref[i], BLOCK), BLOCK), :]
        rows = jnp.where(holds_ref[i] > 0, rows, jnp.zeros_like(rows))
        for c in range(whole):
            start = (c * select + i) * BLOCK
            out_ref[start : start + BLOCK, :] = rows[:, c * wide : (c + 1) * wide]
        out_ref[whole * select * BLOCK :, i * rest : (i + 1) * rest] = rows[:, whole * wide :]


def pick_stored(stored, held_at, holding, wide):
    high = held_at.shape[0] * BLOCK * stored.shape[1] // wide
    return pl.pallas_call(
        pick_kernel,
        in_specs=[
            pl.BlockSpec(memory_space=pltpu.SMEM),
            pl.BlockSpec(memory_space=pltpu.SMEM),
            pl.BlockSpec(memory_space=pltpu.VMEM),
        ],
        out_specs=pl.BlockSpec(memory_space=pltpu.VMEM),
        out_shape=jax.ShapeDtypeStruct((high, wide), jnp.bfloat16),
        cost_estimate=pl.CostEstimate(
            flops=0, bytes_accessed=2 * (stored.size + high * wide), transcendentals=0
        ),
        compiler_params=pltpu.CompilerParams(vmem_limit_bytes=24 * MIB),
    )(held_at, holding.astype(jnp.int32), stored)


def restore(packed, select, hidden):
    wide = packed.shape[1]
    whole = hidden // wide
    rest = hidden - whole * wide
    blocks = []
    for i in range(select):
        cuts = [packed[(c * select + i) * BLOCK :][:BLOCK] for c in range(whole)]
        cuts.append(packed[whole * select * BLOCK :, i * rest : (i + 1) * rest])
        blocks.append(jnp.concatenate(cuts, axis=1))
    return jnp.stack(blocks)


def hidden_kernel(weight_ref, rows_ref, extra_ref, out_ref):
    high = weight_ref.shape[0]
    out_ref[:high, :] = lax.dot_general(
        weight_ref[...],
        rows_ref[...],
        (((1,), (1,)), ((), ())),
        preferred_element_type=jnp.float32,
    ).astype(out_ref.dtype)
    out_ref[high:, :] = extra_ref[...]


def hidden_product(weight, rows, extra, steps):
    high, depth = weight.shape
    slots = rows.shape[0]
    total = high + extra.shape[0]
    return pl.pallas_call(
        hidden_kernel,
        grid=(steps,),
        in_specs=[
            pl.BlockSpec((high // steps, depth), lambda i: (i, 0)),
            pl.BlockSpec((slots, depth), lambda i: (0, 0)),
            pl.BlockSpec((extra.shape[0] // steps, slots), lambda i: (i, 0)),
        ],
        out_specs=pl.BlockSpec((total // steps, slots), lambda i: (i, 0)),
        out_shape=jax.ShapeDtypeStruct((total, slots), jnp.bfloat16),
        cost_estimate=pl.CostEstimate(
            flops=2 * high * depth * slots,
            bytes_accessed=2 * (high * depth + slots * depth + 2 * total * slots),
            transcendentals=0,
        ),
        compiler_params=pltpu.CompilerParams(vmem_limit_bytes=32 * MIB),
    )(weight, rows, extra)


def gates_kernel(rows_ref, grad_ref, *refs):
    weights, own_ref, shown_ref = refs[:-2], refs[-2], refs[-1]
    own_hidden, depth = own_ref.shape[0] // 2, weights[0].shape[1]
    pre = None
    for d, weight in enumerate(weights):
        term = lax.dot_general(
            weight[...],
            rows_ref[:, d * depth : (d + 1) * depth],
            (((1,), (1,)), ((), ())),
            preferred_element_type=jnp.float32,
        )
        pre = term if pre is None else pre + term
    gate_pre, up_pre = pre[:own_hidden], pre[own_hidden:]
    hidden_grad = grad_ref[:own_hidden, :].astype(jnp.float32)
    squashed = 1.0 / (1.0 + jnp.exp(-gate_pre))
    grad_gate = (hidden_grad * up_pre * squashed * (1.0 + gate_pre * (1.0 - squashed))).astype(
        own_ref.dtype
    )
    own_ref[:own_hidden, :] = grad_gate
    own_ref[own_hidden:, :] = (hidden_grad * gate_pre * squashed).astype(own_ref.dtype)
    shown_ref[:own_hidden, :] = grad_gate
    shown_ref[own_hidden:, :] = grad_ref[own_hidden:, :]


def hidden_gates(weights, rows, hidden_grad, tile):
    slots, width = rows.shape
    high, shown = weights[0].shape[0], hidden_grad.shape[0]
    whole = pl.BlockSpec(weights[0].shape, lambda i: (0, 0))
    return pl.pallas_call(
        gates_kernel,
        grid=(slots // tile,),
        in_specs=[
            pl.BlockSpec((tile, width), lambda i: (i, 0)),
            pl.BlockSpec((shown, tile), lambda i: (0, i)),
        ]
        + [whole] * len(weights),
        out_specs=[
            pl.BlockSpec((high, tile), lambda i: (0, i)),
            pl.BlockSpec((shown, tile), lambda i: (0, i)),
        ],
        out_shape=[
            jax.ShapeDtypeStruct((high, slots), jnp.bfloat16),
            jax.ShapeDtypeStruct((shown, slots), jnp.bfloat16),
        ],
        cost_estimate=pl.CostEstimate(
            flops=2 * high * width * slots,
            bytes_accessed=2 * (high * width + slots * width + (high + 2 * shown) * slots),
            transcendentals=high // 2 * slots,
        ),
        compiler_params=pltpu.CompilerParams(vmem_limit_bytes=56 * MIB),
    )(rows, hidden_grad, *weights)


def part_kernel(own_ref, *refs):
    weights, out_ref = refs[:-1], refs[-1]
    depth = weights[0].shape[1]
    own = own_ref[...].T
    for d, weight in enumerate(weights):
        out_ref[:, d * depth : (d + 1) * depth] = jnp.dot(
            own, weight[...], preferred_element_type=jnp.float32
        ).astype(out_ref.dtype)


def slot_parts(own, weights, tile):
    high, slots = own.shape
    width = weights[0].shape[1] * len(weights)
    whole = pl.BlockSpec(weights[0].shape, lambda i: (0, 0))
    return pl.pallas_call(
        part_kernel,
        grid=(slots // tile,),
        in_specs=[pl.BlockSpec((high, tile), lambda i: (0, i))] + [whole] * len(weights),
        out_specs=pl.BlockSpec((tile, width), lambda i: (i, 0)),
        out_shape=jax.ShapeDtypeStruct((slots, width), jnp.bfloat16),
        cost_estimate=pl.CostEstimate(
            flops=2 * high * width * slots,
            bytes_accessed=2 * (high * width + slots * width + high * slots),
            transcendentals=0,
        ),
        compiler_params=pltpu.CompilerParams(vmem_limit_bytes=56 * MIB),
    )(own, *weights)


def combine_kernel(behind_ref, placing_ref, parts_ref, out_ref):
    sides, shares, half, features = out_ref.shape
    for q in range(shares):
        at = pl.ds(pl.multiple_of(behind_ref[q] * features, BLOCK), features)
        rows = jnp.dot(
            placing_ref[...], parts_ref[:, at], preferred_element_type=jnp.float32
        ).astype(out_ref.dtype)
        for j in range(sides):
            out_ref[j, q] = rows[j * half : (j + 1) * half]


def combine(placing, parts, behind, sides):
    tok_rows, slots = placing.shape
    shares = behind.shape[0]
    features = parts.shape[1] // shares
    return pl.pallas_call(
        combine_kernel,
        in_specs=[
            pl.BlockSpec(memory_space=pltpu.SMEM),
            pl.BlockSpec(memory_space=pltpu.VMEM),
            pl.BlockSpec(memory_space=pltpu.VMEM),
        ],
        out_specs=pl.BlockSpec(memory_space=pltpu.VMEM),
        out_shape=jax.ShapeDtypeStruct(
            (sides, shares, tok_rows // sides, features), jnp.bfloat16
        ),
        cost_estimate=pl.CostEstimate(
            flops=2 * slots * tok_rows * features * shares,
            bytes_accessed=2 * (parts.size + placing.size + tok_rows * features * shares),
            transcendentals=0,
        ),
        compiler_params=pltpu.CompilerParams(vmem_limit_bytes=32 * MIB),
    )(behind, placing, parts)


def body(
    tokens,
    cotangent,
    gate_values,
    expert_ids,
    gate_weight,
    up_weight,
    down_weight,
    block_ids,
    feedback,
):
    groups = lax.axis_size("expert")
    shares = lax.axis_size("replica")
    sides = lax.axis_size("tensor")
    here = lax.axis_index("replica")
    experts = groups * gate_weight.shape[0]
    tok_rows, top_count = expert_ids.shape
    capacity = min(tok_rows, tok_rows * top_count * 3 // (2 * experts))
    features = tokens.shape[1]
    width = features * shares
    hidden = gate_weight.shape[2]
    own_hidden = hidden // shares
    stored = feedback[0]

    local_blocks = features // BLOCK
    local_ids = block_ids[0] - here * local_blocks
    holding = jnp.logical_and(local_ids >= 0, local_ids < local_blocks)
    held_at = jnp.clip(local_ids, 0, local_blocks - 1) * BLOCK
    select = local_ids.shape[0]

    pieces = split_weights(gate_weight[0], up_weight[0], here, shares)
    expert_ids, *pieces = lax.optimization_barrier((expert_ids, *pieces))

    def hand_out(d):
        return lax.ppermute(pieces[d], "replica", shift_by(d, shares))

    got = {d: hand_out(d) if d else pieces[0] for d in (0, 4, 3, 5, 2, 6, 1, 7)}

    padded = jnp.pad(tokens, ((0, SPARE), (0, 0)))
    gathered = lax.all_gather(padded, "replica", axis=0, tiled=False)

    placing, slot_gate = routing_tables(expert_ids, gate_values, experts, capacity)
    sent_grads = (
        jnp.dot(placing, cotangent, preferred_element_type=jnp.float32) * slot_gate[:, None]
    ).astype(jnp.bfloat16)
    sent_grads = sent_grads.reshape(experts, capacity, features)
    stored_rows = pick_stored(stored, held_at, holding, experts * capacity)
    sent_grads, stored_rows = lax.optimization_barrier((sent_grads, stored_rows))
    arrived_grads = lax.all_to_all(sent_grads, "expert", split_axis=0, concat_axis=0, tiled=True)
    grad_rows = arrived_grads.reshape(-1, features)
    hidden_part = hidden_product(down_weight[0], grad_rows, stored_rows, shares)
    hidden_part, got[4] = lax.optimization_barrier((hidden_part, got[4]))
    hidden_grad = lax.psum_scatter(hidden_part, "replica", scatter_dimension=0, tiled=True)

    behind = (here - jnp.arange(shares, dtype=jnp.int32)) % shares
    whole_tokens = jnp.take(gathered[:, :tok_rows], behind, axis=0)
    whole_tokens = whole_tokens.transpose(1, 0, 2).reshape(tok_rows, width)
    sent_rows = jnp.dot(placing, whole_tokens, preferred_element_type=jnp.float32)
    sent_rows = sent_rows.astype(jnp.bfloat16).reshape(experts, capacity, width)
    sent_rows, got[3], got[5] = lax.optimization_barrier((sent_rows, got[3], got[5]))
    arrived = lax.all_to_all(sent_rows, "expert", split_axis=0, concat_axis=0, tiled=True)
    slot_rows = arrived.reshape(-1, width)
    weights = [got[d] for d in range(shares)]

    own, shown = hidden_gates(weights, slot_rows, hidden_grad, 2 * BLOCK)
    partial_grad = slot_parts(own, weights, 2 * BLOCK).reshape(experts, capacity, width)
    returned = lax.all_to_all(partial_grad, "expert", split_axis=0, concat_axis=0, tiled=True)

    shown = lax.all_gather(shown, "replica", axis=0, tiled=False)
    grad_gate = shown[:, :own_hidden].reshape(hidden, -1)
    stored_rows = restore(
        shown[:, own_hidden:].reshape(-1, experts * capacity), select, hidden
    )

    gradient = jnp.einsum(
        "sd,fs->df", slot_rows[:, :features], grad_gate, preferred_element_type=jnp.float32
    ) + stored.astype(jnp.float32)
    struck = jnp.any(
        local_ids[:, None] == jnp.arange(local_blocks, dtype=jnp.int32)[None, :], axis=0
    )
    retained = (
        jnp.where(
            struck[:, None, None],
            jnp.float32(0.0),
            gradient.reshape(local_blocks, BLOCK, hidden),
        )
        .reshape(gradient.shape)
        .astype(jnp.bfloat16)
    )

    placed = (here - block_ids[0] // local_blocks) % shares
    picked_at = placed * features + block_ids[0] % local_blocks * BLOCK
    picked = jnp.concatenate(
        [
            lax.dynamic_slice_in_dim(slot_rows, picked_at[i], BLOCK, axis=1)
            for i in range(select)
        ],
        axis=1,
    )
    block_sums = jnp.einsum("sk,fs->kf", picked, grad_gate, preferred_element_type=jnp.float32)
    block_sums = block_sums.reshape(select, BLOCK, hidden) + stored_rows.astype(jnp.float32)
    combined = combine(placing.T, returned.reshape(experts * capacity, width), behind, sides)
    combined = combined.reshape(sides * shares, tok_rows // sides, features)
    collected = lax.all_to_all(
        combined, ("tensor", "replica"), split_axis=0, concat_axis=0, tiled=True
    )
    collected, retained, block_sums = lax.optimization_barrier((collected, retained, block_sums))
    token_grad = jnp.sum(collected.astype(jnp.float32), axis=0).astype(jnp.bfloat16)
    return (token_grad, block_sums[None], retained[None])


def solution(mesh):
    return jax.shard_map(
        body,
        mesh=mesh,
        in_specs=(
            P("expert", "replica"),
            P("expert", "replica"),
            P("expert", None),
            P("expert", None),
            P("expert", "replica", "tensor"),
            P("expert", "replica", "tensor"),
            P("expert", "tensor", "replica"),
            P("expert", None),
            P("expert", "replica", "tensor"),
        ),
        out_specs=(
            P(("expert", "tensor"), "replica"),
            P("expert", None, None, "tensor"),
            P("expert", "replica", "tensor"),
        ),
        check_vma=False,
    )
```

time: 419 us -> 322 us (0.77)
  waiting for transfers between devices: 314 us -> 187 us
  starting transfers between devices: 6.19 us -> 49.8 us
  Pallas kernels: 0 us -> 33.1 us
  blocking collectives: 30 us -> 0 us
  matrix products: 33.6 us -> 12.5 us
  local copies, waits for them, and re-layouts: 4.76 us -> 15.7 us
  other arithmetic: 14 us -> 3.65 us
    reduce_scatter x4 -> x1, waiting for transfers between devices: 158 us -> 7.17 us  [body(): lax.psum_scatter(hidden_part, 'replica', scatter_dimension=0, tiled=True)]
    ppermute x0 -> x7, waiting for transfers between devices: none -> 106 us  [hand_out(): return lax.ppermute(pieces[d], 'replica', shift_by(d, shares))]
    all_gather x2, waiting for transfers between devices: 92.3 us -> 0.04 us  [the longest x1 0.02 us: body(): shown = lax.all_gather(shown, 'replica', axis=0, tiled=False)]
    psum x1 -> x0, waiting for transfers between devices: 53.2 us -> none  [body(): lax.psum(picked.astype(jnp.bfloat16), 'replica').astype(jnp.float32)]
    all_to_all x1, waiting for transfers between devices: 9.8 us -> 58.8 us  [body(): lax.all_to_all(partial_grad, 'expert', split_axis=0, concat_axis=0, tiled...]
    pallas_call x0 -> x6, Pallas kernels: none -> 33.1 us  [the longest x1 9 us: slot_parts(): pl.pallas_call(part_kernel, grid=(slots // tile,), in_specs=[pl.BlockSpec...]
    all_to_all x2 -> x0, blocking collectives: 30 us -> none  [the longest x1 15.9 us: body(): lax.all_to_all(sent_grads, 'expert', split_axis=0, concat_axis=0, tiled=T...]
    ppermute x0 -> x7, starting transfers between devices: none -> 24.9 us  [hand_out(): return lax.ppermute(pieces[d], 'replica', shift_by(d, shares))]
  transfers between devices with their start and end apart: 8 -> 14, of which waited for: 8 -> 10; matrix products, arithmetic and copies ran while one was open for 9% -> 7% of each run, Pallas kernels for 0% -> 8%
where the time goes in v1:
time: 322 us; the launch traced here: 320 us
  waiting for transfers between devices  187 us (58%)
  starting transfers between devices  49.8 us (15%)
  Pallas kernels  33.1 us (10%)
  between operations  17.7 us (5%)
  local copies, waits for them, and re-layouts  15.7 us (5%)
  matrix products  12.5 us (4%)
  other arithmetic  3.65 us (1%)
    ppermute x7, waiting for transfers between devices, hand_out(): return lax.ppermute(pieces[d], 'replica', shift_by(d, shares))  106 us
    all_to_all x1, waiting for transfers between devices, body(): lax.all_to_all(partial_grad, 'expert', split_axis=0, concat_axis=0, tiled...  58.8 us
    ppermute x7, starting transfers between devices, hand_out(): return lax.ppermute(pieces[d], 'replica', shift_by(d, shares))  24.9 us
    all_to_all x1, waiting for transfers between devices, body(): lax.all_to_all(combined, ('tensor', 'replica'), split_axis=0, concat_axis...  12.5 us
    pallas_call x1, Pallas kernels, slot_parts(): pl.pallas_call(part_kernel, grid=(slots // tile,), in_specs=[pl.BlockSpec...  9 us
    pallas_call x1, Pallas kernels, hidden_gates(): pl.pallas_call(gates_kernel, grid=(slots // tile,), in_specs=[pl.BlockSpe...  8.58 us
    all_to_all x1, starting transfers between devices, body(): lax.all_to_all(sent_rows, 'expert', split_axis=0, concat_axis=0, tiled=True)  7.17 us
    reduce_scatter x1, waiting for transfers between devices, body(): lax.psum_scatter(hidden_part, 'replica', scatter_dimension=0, tiled=True)  7.17 us
  transfers between devices with their start and end apart: 14, of which 10 were waited for; matrix products, arithmetic and copies ran while one was open for 7% of the time, Pallas kernels for 8%

profile of v1, /device:TPU:8, one launch (start us, length us, event | category | flops | bytes accessed | tf_op | source)
XLA Modules:
  0.0 319.9 jit_solution(9726293406029383971)
XLA Ops:
  7.2 1.6 pad.4
  8.8 6.9 %shard_map.112 = (bf16[672,384]{1,0:T(8,128)(2,1)}, bf16[672,384]{1,0:T(8,128)(2,1)}, bf16[672,384]{1,0:T(8,128)(2,1)}, bf16[672,384]{1,0:T(8,128)(2,1)}, bf16[6...) custom-call(s32[1]{0:T(128)} %bitcast.refs_0_, ...), custom_call_target="tpu_custom_call" | custom-call | bytes 8257536 | tf_op jit(solution)/shard_map/pallas_call | solution.py:53
  16.1 1.2 reduce-window.6
  17.3 0.2 slice_reduce_fusion
  17.9 0.7 shard_map.113.extra_ref
  18.6 0.2 fusion.2
  18.8 0.9 select_reduce_fusion
  19.7 1.1 fusion.3
  20.9 5.8 %all-to-all-start.1 = ((bf16[16,48,384]{2,1,0:T(8,128)(2,1)}), bf16[16,48,384]{2,1,0:T(8,128)(2,1)S(1)}, u32[]{:S(2)}, u32[]{:S(2)}) async-start(bf16[16,48,384]{2,1,0:T(8,128)(2,1)} %bitcast.12), calls=%async_computation.1 | async-start | bytes 1179648 | tf_op jit(solution)/shard_map/all_to_all | solution.py:312
  26.7 7.3 %collective-permute-start.2 = (bf16[672,384]{1,0:T(8,128)(2,1)}, bf16[672,384]{1,0:T(8,128)(2,1)S(1)}, u32[]{:S(2)}, u32[]{:S(2)}) collective-permute-start(bf16[672,384]{1,0:T(8,128)(2,1)} %get-tuple-element.46), channel_id=1, source_target_pairs={{0,4},{1,5},{2,6},{3,7},{4,0},{5,1},{6,2},{7,3},{8,12},{9,13},{10,... | collective-permute-start | bytes 1548296 | tf_op jit(solution)/shard_map/ppermute | solution.py:298
  34.0 2.7 all-to-all-done.1
  36.7 1.6 copy-done.5
  38.3 3.7 %shard_map.114 = bf16[3584,768]{1,0:T(8,128)(2,1)S(1)} custom-call(bf16[2688,384]{1,0:T(8,128)(2,1)S(1)} %bitcast.85, bf16[768,384]{1,0:T(8,128)(2,1)S(1)} %bitcast.83, bf16[896,768]{1,0:T(8,128)(2,1)S(1)} %shard_map.113.extra_ref), custom_call_target="tpu_custom_call" | custom-call | flops 1585446912 | bytes 13664256 | tf_op jit(solution)/shard_map/pallas_call | solution.py:128
  42.0 2.4 copy-done.2
  44.3 14.0 %collective-permute-done.2.refs_4_ = bf16[672,384]{1,0:T(8,128)(2,1)S(1)} collective-permute-done((bf16[672,384]{1,0:T(8,128)(2,1)}, bf16[672,384]{1,0:T(8,128)(2,1)S(1)}, u32[]{:S(2)}, u32[]{:S(2)}) %collective-permute-start.2) | collective-permute-done | bytes 516128 | tf_op jit(solution)/shard_map/ppermute | solution.py:298
  58.3 0.8 copy-done.13
  59.1 6.7 %collective-permute-start = (bf16[672,384]{1,0:T(8,128)(2,1)S(1)}, bf16[672,384]{1,0:T(8,128)(2,1)S(1)}, u32[]{:S(2)}, u32[]{:S(2)}) collective-permute-start(bf16[672,384]{1,0:T(8,128)(2,1)S(1)} %copy-done.15), channel_id=1, source_target_pairs={{0,3},{1,4},{2,5},{3,6},{4,7},{5,0},{6,1},{7,2},{8,11},{9,12},{10,... | collective-permute-start | bytes 1548296 | tf_op jit(solution)/shard_map/ppermute | solution.py:298
  65.9 3.1 collective-permute-start.1
  69.0 1.2 slice.77
  70.3 0.7 gather_fusion
  71.2 0.4 copy.44
  71.5 3.6 %convolution_convert_fusion = bf16[768,3072]{1,0:T(8,128)(2,1)} fusion(pred[768,128]{1,0:T(8,128)(4,1)S(1)} %fusion.2, bf16[128,3072]{0,1:T(8,128)(2,1)S(1)} %bitcast.94), kind=kOutput, calls=%fused_computation.1 | convolution fusion | flops 606339072 | bytes 5603328 | tf_op jit(solution)/shard_map/dot_general | solution.py:321
  75.2 34.2 %collective-permute-done.refs_3_ = bf16[672,384]{1,0:T(8,128)(2,1)S(1)} collective-permute-done((bf16[672,384]{1,0:T(8,128)(2,1)S(1)}, bf16[672,384]{1,0:T(8,128)(2,1)S(1)}, u32[]{:S(2)}, u32[]{:S(2)}) %collective-permute-start) | collective-permute-done | bytes 516128 | tf_op jit(solution)/shard_map/ppermute | solution.py:298
  109.4 1.5 collective-permute-done.1.refs_5_
  110.9 7.2 %all-to-all-start = ((bf16[16,48,3072]{2,1,0:T(8,128)(2,1)}), bf16[16,48,3072]{2,1,0:T(8,128)(2,1)}, u32[]{:S(2)}, u32[]{:S(2)}) async-start(bf16[16,48,3072]{2,1,0:T(8,128)(2,1)} %bitcast.86), calls=%async_computation | async-start | bytes 9437184 | tf_op jit(solution)/shard_map/all_to_all | solution.py:324
  118.2 4.9 %collective-permute-start.4 = (bf16[672,384]{1,0:T(8,128)(2,1)S(1)}, bf16[672,384]{1,0:T(8,128)(2,1)S(1)}, u32[]{:S(2)}, u32[]{:S(2)}) collective-permute-start(bf16[672,384]{1,0:T(8,128)(2,1)S(1)} %copy-done.11), channel_id=1, source_target_pairs={{0,2},{1,3},{2,4},{3,5},{4,6},{5,7},{6,0},{7,1},{8,10},{9,11},{10,... | collective-permute-start | bytes 1548296 | tf_op jit(solution)/shard_map/ppermute | solution.py:298
  123.1 0.4 collective-permute-start.5
  123.5 2.4 collective-permute-start.6
  125.9 19.7 %collective-permute-done.3.refs_1_ = bf16[672,384]{1,0:T(8,128)(2,1)S(1)} collective-permute-done((bf16[672,384]{1,0:T(8,128)(2,1)S(1)}, bf16[672,384]{1,0:T(8,128)(2,1)S(1)}, u32[]{:S(2)}, u32[]{:S(2)}) %collective-permute-start.3) | collective-permute-done | bytes 516128 | tf_op jit(solution)/shard_map/ppermute | solution.py:298
  145.6 33.1 %collective-permute-done.4.refs_2_ = bf16[672,384]{1,0:T(8,128)(2,1)S(1)} collective-permute-done((bf16[672,384]{1,0:T(8,128)(2,1)S(1)}, bf16[672,384]{1,0:T(8,128)(2,1)S(1)}, u32[]{:S(2)}, u32[]{:S(2)}) %collective-permute-start.4) | collective-permute-done | bytes 516128 | tf_op jit(solution)/shard_map/ppermute | solution.py:298
  178.8 0.8 copy-done.19
  179.6 3.5 %collective-permute-done.6.refs_7_ = bf16[672,384]{1,0:T(8,128)(2,1)} collective-permute-done((bf16[672,384]{1,0:T(8,128)(2,1)S(1)}, bf16[672,384]{1,0:T(8,128)(2,1)}, u32[]{:S(2)}, u32[]{:S(2)}) %collective-permute-start.6) | collective-permute-done | bytes 516128 | tf_op jit(solution)/shard_map/ppermute | solution.py:298
  183.1 7.2 %reduce-scatter.2.cloned.1.call-done.grad_ref = bf16[448,768]{1,0:T(8,128)(2,1)} async-done(((bf16[3584,768]{1,0:T(8,128)(2,1)}), bf16[448,768]{1,0:T(8,128)(2,1)}) %reduce-scatter.2.cloned.1.call-update) | async-done | bytes 688144 | tf_op jit(solution)/shard_map/reduce_scatter | solution.py:316
  190.3 8.6 %shard_map.115 = (bf16[672,768]{1,0:T(8,128)(2,1)}, bf16[448,768]{1,0:T(8,128)(2,1)}) custom-call(bf16[768,3072]{1,0:T(8,128)(2,1)} %bitcast.10.rows_ref, bf16[448,768]{1,0:T(8,128)(2,1)} %reduce-scatter.2.cloned.1.call-done.grad_ref, bf16[672,384]{1,0:T(8,128)(2,1)} %get-tuple-element.48.refs_0_, bf16[672,384]{1,0:T(8,128)(2,1)} %copy-done.17, ...), custom_call_target="tpu_custom_call" | custom-call | flops 3170893824 | bytes 11255808 | tf_op jit(solution)/shard_map/pallas_call | solution.py:175
  198.9 9.0 %shard_map.116 = bf16[768,3072]{1,0:T(8,128)(2,1)} custom-call(bf16[672,768]{1,0:T(8,128)(2,1)} %get-tuple-element.56.own_ref, bf16[672,384]{1,0:T(8,128)(2,1)} %get-tuple-element.48.refs_0_, bf16[672,384]{1,0:T(8,128)(2,1)} %copy-done.17, bf16[672,384]{1,0:T(8,128)(2,1)} %copy-done.18, bf16[672,384]{1,0:T(8,128)(2,1)} %copy-done.16, ...), custom_call_target="tpu_custom_call" | custom-call | flops 3170893824 | bytes 9879552 | tf_op jit(solution)/shard_map/pallas_call | solution.py:214
  207.9 5.5 %all-to-all-start.2 = ((bf16[16,48,3072]{2,1,0:T(8,128)(2,1)}), bf16[16,48,3072]{2,1,0:T(8,128)(2,1)}, u32[]{:S(2)}, u32[]{:S(2)}) async-start(bf16[16,48,3072]{2,1,0:T(8,128)(2,1)} %bitcast.93), calls=%async_computation.3 | async-start | bytes 9437184 | tf_op jit(solution)/shard_map/all_to_all | solution.py:330
  213.6 0.6 fusion.19
  218.0 1.3 constant_dynamic-slice_fusion.1
  219.6 58.8 %all-to-all-done.2 = bf16[16,48,3072]{2,1,0:T(8,128)(2,1)} async-done(((bf16[16,48,3072]{2,1,0:T(8,128)(2,1)}), bf16[16,48,3072]{2,1,0:T(8,128)(2,1)}, u32[]{:S(2)}, u32[]{:S(2)}) %all-to-all-start.2) | async-done | bytes 4718624 | tf_op jit(solution)/shard_map/all_to_all | solution.py:330
  278.4 4.2 %shard_map.117 = bf16[2,8,64,384]{3,2,1,0:T(8,128)(2,1)} custom-call(s32[8]{0:T(128)S(1)} %and_select_fusion.3.behind_ref, bf16[128,768]{1,0:T(8,128)(2,1)S(1)} %convert_bitcast_fusion.placing_ref, bf16[768,3072]{1,0:T(8,128)(2,1)} %bitcast.17.parts_ref), custom_call_target="tpu_custom_call" | custom-call | flops 603979776 | bytes 5701632 | tf_op jit(solution)/shard_map/pallas_call | solution.py:244
  282.6 6.4 %all-to-all-start.3 = ((bf16[16,64,384]{2,1,0:T(8,128)(2,1)}), bf16[16,64,384]{2,1,0:T(8,128)(2,1)S(1)}, u32[]{:S(2)}, u32[]{:S(2)}) async-start(bf16[16,64,384]{2,1,0:T(8,128)(2,1)} %bitcast.18), calls=%async_computation.4 | async-start | bytes 1572864 | tf_op jit(solution)/shard_map/all_to_all | solution.py:367
  289.1 1.6 slice.80
  290.9 1.2 copy-done.6
  292.1 0.3 slice.79
  292.4 2.9 convolution_add_fusion.1
  295.3 4.8 %fusion.1 = bf16[384,2688]{1,0:T(8,128)(2,1)} fusion(bf16[2688,768]{1,0:T(8,128)(2,1)S(1)} %bitcast.88, pred[384]{0:T(512)(128)(4,1)S(1)} %broadcast_bitcast_fusion, bf16[768,3072]{1,0:T(8,128)(2,1)} %bitcast.10.rows_ref, bf16[1,384,2688]{2,1,0:T(8,128)(2,1)S(1)} %copy-done.4), kind=kOutput, calls=%fused_computation.4 | convolution fusion | flops 1589575680 | bytes 8847744 | tf_op jit(solution)/shard_map/sd,fs->df/dot_general | solution.py:338
  300.1 12.5 %all-to-all-done.3 = bf16[16,64,384]{2,1,0:T(8,128)(2,1)S(1)} async-done(((bf16[16,64,384]{2,1,0:T(8,128)(2,1)}), bf16[16,64,384]{2,1,0:T(8,128)(2,1)S(1)}, u32[]{:S(2)}, u32[]{:S(2)}) %all-to-all-start.3) | async-done | bytes 786464 | tf_op jit(solution)/shard_map/all_to_all | solution.py:367
  312.6 0.7 reduce_sum.35
  (73 shorter events, 2.1 us)
Async XLA Ops:
  7.2 12.6 %copy-start = (bf16[128,384]{1,0:T(8,128)(2,1)S(1)}, bf16[128,384]{1,0:T(8,128)(2,1)}, u32[]{:S(2)}) copy-start(bf16[128,384]{1,0:T(8,128)(2,1)} %param.10) | copy-start | bytes 294916
  7.2 61.8 %all-gather.5.cloned.1.call-start = ((), (), s32[]{:S(2)}) async-start(), calls=%async_computation.6 | async-start | bytes 1216512 | tf_op jit(solution)/shard_map/all_gather | solution.py:303
  8.8 6.9 %copy-start.7 = (s32[128,4]{0,1:T(4,128)S(1)}, s32[128,4]{0,1:T(4,128)}, u32[]{:S(2)}) copy-start(s32[128,4]{0,1:T(4,128)} %param.12) | copy-start | bytes 6148
  8.8 9.0 %copy-start.8 = (s32[1,2]{1,0:T(1,128)S(1)}, s32[1,2]{1,0:T(1,128)}, u32[]{:S(2)}) copy-start(s32[1,2]{1,0:T(1,128)} %param.16) | copy-start | bytes 28
  8.8 9.0 %copy-start.3 = (bf16[1,384,2688]{2,1,0:T(8,128)(2,1)S(1)}, bf16[1,384,2688]{2,1,0:T(8,128)(2,1)}, u32[]{:S(2)}) copy-start(bf16[1,384,2688]{2,1,0:T(8,128)(2,1)} %param.17) | copy-start | bytes 6193156
  20.9 15.8 %all-to-all-start.1 = ((bf16[16,48,384]{2,1,0:T(8,128)(2,1)}), bf16[16,48,384]{2,1,0:T(8,128)(2,1)S(1)}, u32[]{:S(2)}, u32[]{:S(2)}) async-start(bf16[16,48,384]{2,1,0:T(8,128)(2,1)} %bitcast.12), calls=%async_computation.1 | async-start | bytes 1179648 | tf_op jit(solution)/shard_map/all_to_all | solution.py:312
  26.7 163.6 %reduce-scatter.2.cloned.1.call-start = ((), (), s32[]{:S(2)}) async-start(), calls=%async_computation.5 | async-start | bytes 6193152 | tf_op jit(solution)/shard_map/reduce_scatter | solution.py:316
  26.7 31.6 %collective-permute-start.2 = (bf16[672,384]{1,0:T(8,128)(2,1)}, bf16[672,384]{1,0:T(8,128)(2,1)S(1)}, u32[]{:S(2)}, u32[]{:S(2)}) collective-permute-start(bf16[672,384]{1,0:T(8,128)(2,1)} %get-tuple-element.46), channel_id=1, source_target_pairs={{0,4},{1,5},{2,6},{3,7},{4,0},{5,1},{6,2},{7,3},{8,12},{9,13},{10,... | collective-permute-start | bytes 1548296 | tf_op jit(solution)/shard_map/ppermute | solution.py:298
  36.7 1.6 copy-start.5
  42.0 2.4 copy-start.2
  44.3 14.8 %copy-start.15 = (bf16[672,384]{1,0:T(8,128)(2,1)S(1)}, bf16[672,384]{1,0:T(8,128)(2,1)}, u32[]{:S(2)}) copy-start(bf16[672,384]{1,0:T(8,128)(2,1)} %get-tuple-element.41) | copy-start | bytes 1548292
  44.3 21.5 %copy-start.14 = (bf16[672,384]{1,0:T(8,128)(2,1)S(1)}, bf16[672,384]{1,0:T(8,128)(2,1)}, u32[]{:S(2)}) copy-start(bf16[672,384]{1,0:T(8,128)(2,1)} %get-tuple-element.42) | copy-start | bytes 1548292
  58.3 0.8 copy-start.13
  59.1 50.2 %collective-permute-start = (bf16[672,384]{1,0:T(8,128)(2,1)S(1)}, bf16[672,384]{1,0:T(8,128)(2,1)S(1)}, u32[]{:S(2)}, u32[]{:S(2)}) collective-permute-start(bf16[672,384]{1,0:T(8,128)(2,1)S(1)} %copy-done.15), channel_id=1, source_target_pairs={{0,3},{1,4},{2,5},{3,6},{4,7},{5,0},{6,1},{7,2},{8,11},{9,12},{10,... | collective-permute-start | bytes 1548296 | tf_op jit(solution)/shard_map/ppermute | solution.py:298
  65.9 45.0 %collective-permute-start.1 = (bf16[672,384]{1,0:T(8,128)(2,1)S(1)}, bf16[672,384]{1,0:T(8,128)(2,1)}, u32[]{:S(2)}, u32[]{:S(2)}) collective-permute-start(bf16[672,384]{1,0:T(8,128)(2,1)S(1)} %copy-done.14), channel_id=1, source_target_pairs={{0,5},{1,6},{2,7},{3,0},{4,1},{5,2},{6,3},{7,4},{8,13},{9,14},{10,... | collective-permute-start | bytes 1548296 | tf_op jit(solution)/shard_map/ppermute | solution.py:298
  109.4 1.5 copy-start.16
  110.9 7.2 %copy-start.12 = (bf16[672,384]{1,0:T(8,128)(2,1)S(1)}, bf16[672,384]{1,0:T(8,128)(2,1)}, u32[]{:S(2)}) copy-start(bf16[672,384]{1,0:T(8,128)(2,1)} %get-tuple-element.49) | copy-start | bytes 1548292
  110.9 7.3 %copy-start.11 = (bf16[672,384]{1,0:T(8,128)(2,1)S(1)}, bf16[672,384]{1,0:T(8,128)(2,1)}, u32[]{:S(2)}) copy-start(bf16[672,384]{1,0:T(8,128)(2,1)} %get-tuple-element.50) | copy-start | bytes 1548292
  110.9 12.2 %copy-start.10 = (bf16[672,384]{1,0:T(8,128)(2,1)S(1)}, bf16[672,384]{1,0:T(8,128)(2,1)}, u32[]{:S(2)}) copy-start(bf16[672,384]{1,0:T(8,128)(2,1)} %get-tuple-element.54) | copy-start | bytes 1548292
  110.9 12.6 %copy-start.9 = (bf16[672,384]{1,0:T(8,128)(2,1)S(1)}, bf16[672,384]{1,0:T(8,128)(2,1)}, u32[]{:S(2)}) copy-start(bf16[672,384]{1,0:T(8,128)(2,1)} %get-tuple-element.55) | copy-start | bytes 1548292
  110.9 72.2 %all-to-all-start = ((bf16[16,48,3072]{2,1,0:T(8,128)(2,1)}), bf16[16,48,3072]{2,1,0:T(8,128)(2,1)}, u32[]{:S(2)}, u32[]{:S(2)}) async-start(bf16[16,48,3072]{2,1,0:T(8,128)(2,1)} %bitcast.86), calls=%async_computation | async-start | bytes 9437184 | tf_op jit(solution)/shard_map/all_to_all | solution.py:324
  118.1 171.0 %all-gather.7.cloned.1.call-start = ((), (), s32[]{:S(2)}) async-start(), calls=%async_computation.7 | async-start | bytes 6193152 | tf_op jit(solution)/shard_map/all_gather | solution.py:332
  118.1 27.5 %collective-permute-start.3 = (bf16[672,384]{1,0:T(8,128)(2,1)S(1)}, bf16[672,384]{1,0:T(8,128)(2,1)S(1)}, u32[]{:S(2)}, u32[]{:S(2)}) collective-permute-start(bf16[672,384]{1,0:T(8,128)(2,1)S(1)} %copy-done.12), channel_id=1, source_target_pairs={{0,1},{1,2},{2,3},{3,4},{4,5},{5,6},{6,7},{7,0},{8,9},{9,10},{10,1... | collective-permute-start | bytes 1548296 | tf_op jit(solution)/shard_map/ppermute | solution.py:298
  118.2 60.5 %collective-permute-start.4 = (bf16[672,384]{1,0:T(8,128)(2,1)S(1)}, bf16[672,384]{1,0:T(8,128)(2,1)S(1)}, u32[]{:S(2)}, u32[]{:S(2)}) collective-permute-start(bf16[672,384]{1,0:T(8,128)(2,1)S(1)} %copy-done.11), channel_id=1, source_target_pairs={{0,2},{1,3},{2,4},{3,5},{4,6},{5,7},{6,0},{7,1},{8,10},{9,11},{10,... | collective-permute-start | bytes 1548296 | tf_op jit(solution)/shard_map/ppermute | solution.py:298
  123.1 55.7 %collective-permute-start.5 = (bf16[672,384]{1,0:T(8,128)(2,1)S(1)}, bf16[672,384]{1,0:T(8,128)(2,1)S(1)}, u32[]{:S(2)}, u32[]{:S(2)}) collective-permute-start(bf16[672,384]{1,0:T(8,128)(2,1)S(1)} %copy-done.10), channel_id=1, source_target_pairs={{0,6},{1,7},{2,0},{3,1},{4,2},{5,3},{6,4},{7,5},{8,14},{9,15},{10,... | collective-permute-start | bytes 1548296 | tf_op jit(solution)/shard_map/ppermute | solution.py:298
  123.5 59.6 %collective-permute-start.6 = (bf16[672,384]{1,0:T(8,128)(2,1)S(1)}, bf16[672,384]{1,0:T(8,128)(2,1)}, u32[]{:S(2)}, u32[]{:S(2)}) collective-permute-start(bf16[672,384]{1,0:T(8,128)(2,1)S(1)} %copy-done.9), channel_id=1, source_target_pairs={{0,7},{1,0},{2,1},{3,2},{4,3},{5,4},{6,5},{7,6},{8,15},{9,8},{10,9... | collective-permute-start | bytes 1548296 | tf_op jit(solution)/shard_map/ppermute | solution.py:298
  145.6 44.7 %copy-start.17 = (bf16[672,384]{1,0:T(8,128)(2,1)}, bf16[672,384]{1,0:T(8,128)(2,1)S(1)}, u32[]{:S(2)}) copy-start(bf16[672,384]{1,0:T(8,128)(2,1)S(1)} %collective-permute-done.3.refs_1_) | copy-start | bytes 1548292
  178.8 11.5 %copy-start.18 = (bf16[672,384]{1,0:T(8,128)(2,1)}, bf16[672,384]{1,0:T(8,128)(2,1)S(1)}, u32[]{:S(2)}) copy-start(bf16[672,384]{1,0:T(8,128)(2,1)S(1)} %collective-permute-done.4.refs_2_) | copy-start | bytes 1548292
  178.8 0.8 copy-start.19
  207.9 70.5 %all-to-all-start.2 = ((bf16[16,48,3072]{2,1,0:T(8,128)(2,1)}), bf16[16,48,3072]{2,1,0:T(8,128)(2,1)}, u32[]{:S(2)}, u32[]{:S(2)}) async-start(bf16[16,48,3072]{2,1,0:T(8,128)(2,1)} %bitcast.93), calls=%async_computation.3 | async-start | bytes 9437184 | tf_op jit(solution)/shard_map/all_to_all | solution.py:330
  282.6 30.0 %all-to-all-start.3 = ((bf16[16,64,384]{2,1,0:T(8,128)(2,1)}), bf16[16,64,384]{2,1,0:T(8,128)(2,1)S(1)}, u32[]{:S(2)}, u32[]{:S(2)}) async-start(bf16[16,64,384]{2,1,0:T(8,128)(2,1)} %bitcast.18), calls=%async_computation.4 | async-start | bytes 1572864 | tf_op jit(solution)/shard_map/all_to_all | solution.py:367
  289.1 3.0 copy-start.6
  292.4 2.9 copy-start.4
  295.3 18.1 %copy-start.1 = (bf16[128,384]{1,0:T(8,128)(2,1)S(1)}, bf16[128,384]{1,0:T(8,128)(2,1)}, u32[]{:S(2)}) copy-start(bf16[128,384]{1,0:T(8,128)(2,1)} %param.10) | copy-start | bytes 294916
Sparse Core Ops, SparseCore 0:
  9.8 51.3 all-gather.4
  63.7 126.5 reduce-scatter.1
  199.0 65.7 all-gather.6

commit v2 on v1

--- a/solution.py
+++ b/solution.py
@@ -98,41 +98,69 @@
     )(held_at, holding.astype(jnp.int32), stored)
 
 
-def restore(packed, select, hidden):
-    wide = packed.shape[1]
+def restore_kernel(products_ref, packed_ref, out_ref):
+    select, _, hidden = out_ref.shape
+    wide = packed_ref.shape[1]
     whole = hidden // wide
     rest = hidden - whole * wide
-    blocks = []
     for i in range(select):
-        cuts = [packed[(c * select + i) * BLOCK :][:BLOCK] for c in range(whole)]
-        cuts.append(packed[whole * select * BLOCK :, i * rest : (i + 1) * rest])
-        blocks.append(jnp.concatenate(cuts, axis=1))
-    return jnp.stack(blocks)
-
-
-def hidden_kernel(weight_ref, rows_ref, extra_ref, out_ref):
-    high = weight_ref.shape[0]
+        at = slice(i * BLOCK, (i + 1) * BLOCK)
+        for c in range(whole):
+            start, columns = (c * select + i) * BLOCK, slice(c * wide, (c + 1) * wide)
+            out_ref[i, :, columns] = products_ref[at, columns] + packed_ref[
+                start : start + BLOCK, :
+            ].astype(jnp.float32)
+        out_ref[i, :, whole * wide :] = products_ref[at, whole * wide :] + packed_ref[
+            whole * select * BLOCK :, i * rest : (i + 1) * rest
+        ].astype(jnp.float32)
+
+
+def add_stored(products, shown, at, select):
+    hidden = products.shape[1]
+    wide = shown.shape[1] // (at + 1)
+    return pl.pallas_call(
+        restore_kernel,
+        grid=(1,),
+        in_specs=[
+            pl.BlockSpec((select * BLOCK, hidden), lambda i: (0, 0)),
+            pl.BlockSpec((shown.shape[0], wide), lambda i: (0, at)),
+        ],
+        out_specs=pl.BlockSpec((select, BLOCK, hidden), lambda i: (0, 0, 0)),
+        out_shape=jax.ShapeDtypeStruct((select, BLOCK, hidden), jnp.float32),
+        cost_estimate=pl.CostEstimate(
+            flops=select * BLOCK * hidden,
+            bytes_accessed=10 * select * BLOCK * hidden,
+            transcendentals=0,
+        ),
+        compiler_params=pltpu.CompilerParams(vmem_limit_bytes=32 * MIB),
+    )(products, shown)
+
+
+def hidden_kernel(weight_ref, rows_ref, *refs):
+    out_ref, high = refs[-1], weight_ref.shape[0]
     out_ref[:high, :] = lax.dot_general(
         weight_ref[...],
         rows_ref[...],
         (((1,), (1,)), ((), ())),
         preferred_element_type=jnp.float32,
     ).astype(out_ref.dtype)
-    out_ref[high:, :] = extra_ref[...]
+    if len(refs) > 1:
+        out_ref[high:, :] = refs[0][...]
 
 
 def hidden_product(weight, rows, extra, steps):
     high, depth = weight.shape
     slots = rows.shape[0]
-    total = high + extra.shape[0]
+    more = [] if extra is None else [extra]
+    total = high + sum(e.shape[0] for e in more)
     return pl.pallas_call(
         hidden_kernel,
         grid=(steps,),
         in_specs=[
             pl.BlockSpec((high // steps, depth), lambda i: (i, 0)),
             pl.BlockSpec((slots, depth), lambda i: (0, 0)),
-            pl.BlockSpec((extra.shape[0] // steps, slots), lambda i: (i, 0)),
-        ],
+        ]
+        + [pl.BlockSpec((e.shape[0] // steps, slots), lambda i: (i, 0)) for e in more],
         out_specs=pl.BlockSpec((total // steps, slots), lambda i: (i, 0)),
         out_shape=jax.ShapeDtypeStruct((total, slots), jnp.bfloat16),
         cost_estimate=pl.CostEstimate(
@@ -141,56 +169,50 @@
             transcendentals=0,
         ),
         compiler_params=pltpu.CompilerParams(vmem_limit_bytes=32 * MIB),
-    )(weight, rows, extra)
+    )(weight, rows, *more)
 
 
 def gates_kernel(rows_ref, grad_ref, *refs):
-    weights, own_ref, shown_ref = refs[:-2], refs[-2], refs[-1]
+    weights, own_ref = refs[:-1], refs[-1]
     own_hidden, depth = own_ref.shape[0] // 2, weights[0].shape[1]
+    slots = own_ref.shape[1]
     pre = None
     for d, weight in enumerate(weights):
         term = lax.dot_general(
             weight[...],
-            rows_ref[:, d * depth : (d + 1) * depth],
+            rows_ref[:, :, :, d * depth : (d + 1) * depth].reshape(slots, depth),
             (((1,), (1,)), ((), ())),
             preferred_element_type=jnp.float32,
         )
         pre = term if pre is None else pre + term
     gate_pre, up_pre = pre[:own_hidden], pre[own_hidden:]
-    hidden_grad = grad_ref[:own_hidden, :].astype(jnp.float32)
+    hidden_grad = grad_ref[...].astype(jnp.float32)
     squashed = 1.0 / (1.0 + jnp.exp(-gate_pre))
-    grad_gate = (hidden_grad * up_pre * squashed * (1.0 + gate_pre * (1.0 - squashed))).astype(
-        own_ref.dtype
-    )
-    own_ref[:own_hidden, :] = grad_gate
+    own_ref[:own_hidden, :] = (
+        hidden_grad * up_pre * squashed * (1.0 + gate_pre * (1.0 - squashed))
+    ).astype(own_ref.dtype)
     own_ref[own_hidden:, :] = (hidden_grad * gate_pre * squashed).astype(own_ref.dtype)
-    shown_ref[:own_hidden, :] = grad_gate
-    shown_ref[own_hidden:, :] = grad_ref[own_hidden:, :]
-
-
-def hidden_gates(weights, rows, hidden_grad, tile):
-    slots, width = rows.shape
-    high, shown = weights[0].shape[0], hidden_grad.shape[0]
+
+
+def hidden_gates(weights, rows, first, count, hidden_grad, at, tile):
+    groups, _, low, width = rows.shape
+    high, slots = weights[0].shape[0], groups * count * low
+    own_hidden = high // 2
+    block = (tile // (count * low), count, low, width)
     whole = pl.BlockSpec(weights[0].shape, lambda i: (0, 0))
     return pl.pallas_call(
         gates_kernel,
         grid=(slots // tile,),
         in_specs=[
-            pl.BlockSpec((tile, width), lambda i: (i, 0)),
-            pl.BlockSpec((shown, tile), lambda i: (0, i)),
+            pl.BlockSpec(block, lambda i: (i, first // count, 0, 0)),
+            pl.BlockSpec((own_hidden, tile), lambda i: (0, at + i)),
         ]
         + [whole] * len(weights),
-        out_specs=[
-            pl.BlockSpec((high, tile), lambda i: (0, i)),
-            pl.BlockSpec((shown, tile), lambda i: (0, i)),
-        ],
-        out_shape=[
-            jax.ShapeDtypeStruct((high, slots), jnp.bfloat16),
-            jax.ShapeDtypeStruct((shown, slots), jnp.bfloat16),
-        ],
+        out_specs=pl.BlockSpec((high, tile), lambda i: (0, i)),
+        out_shape=jax.ShapeDtypeStruct((high, slots), jnp.bfloat16),
         cost_estimate=pl.CostEstimate(
             flops=2 * high * width * slots,
-            bytes_accessed=2 * (high * width + slots * width + (high + 2 * shown) * slots),
+            bytes_accessed=2 * (high * width + slots * width + 2 * high * slots),
             transcendentals=high // 2 * slots,
         ),
         compiler_params=pltpu.CompilerParams(vmem_limit_bytes=56 * MIB),
@@ -226,39 +248,41 @@
     )(own, *weights)
 
 
-def combine_kernel(behind_ref, placing_ref, parts_ref, out_ref):
+def combine_kernel(behind_ref, *refs):
+    out_ref, half_refs = refs[-1], refs[:-1]
     sides, shares, half, features = out_ref.shape
     for q in range(shares):
         at = pl.ds(pl.multiple_of(behind_ref[q] * features, BLOCK), features)
-        rows = jnp.dot(
-            placing_ref[...], parts_ref[:, at], preferred_element_type=jnp.float32
-        ).astype(out_ref.dtype)
+        rows = jnp.zeros((sides * half, features), jnp.float32)
+        for placing_ref, parts_ref in zip(half_refs[::2], half_refs[1::2]):
+            rows = rows + jnp.dot(
+                placing_ref[...], parts_ref[:, at], preferred_element_type=jnp.float32
+            )
+        rows = rows.astype(out_ref.dtype)
         for j in range(sides):
             out_ref[j, q] = rows[j * half : (j + 1) * half]
 
 
-def combine(placing, parts, behind, sides):
-    tok_rows, slots = placing.shape
+def combine(pairs, behind, sides):
+    tok_rows = pairs[0][0].shape[0]
+    width = pairs[0][1].shape[1]
+    slots = sum(placing.shape[1] for placing, _ in pairs)
     shares = behind.shape[0]
-    features = parts.shape[1] // shares
     return pl.pallas_call(
         combine_kernel,
-        in_specs=[
-            pl.BlockSpec(memory_space=pltpu.SMEM),
-            pl.BlockSpec(memory_space=pltpu.VMEM),
-            pl.BlockSpec(memory_space=pltpu.VMEM),
-        ],
+        in_specs=[pl.BlockSpec(memory_space=pltpu.SMEM)]
+        + [pl.BlockSpec(memory_space=pltpu.VMEM)] * (2 * len(pairs)),
         out_specs=pl.BlockSpec(memory_space=pltpu.VMEM),
         out_shape=jax.ShapeDtypeStruct(
-            (sides, shares, tok_rows // sides, features), jnp.bfloat16
-        ),
-        cost_estimate=pl.CostEstimate(
-            flops=2 * slots * tok_rows * features * shares,
-            bytes_accessed=2 * (parts.size + placing.size + tok_rows * features * shares),
+            (sides, shares, tok_rows // sides, width // shares), jnp.bfloat16
+        ),
+        cost_estimate=pl.CostEstimate(
+            flops=2 * slots * tok_rows * width,
+            bytes_accessed=2 * (slots * width + slots * tok_rows + tok_rows * width),
             transcendentals=0,
         ),
         compiler_params=pltpu.CompilerParams(vmem_limit_bytes=32 * MIB),
-    )(behind, placing, parts)
+    )(behind, *[array for pair in pairs for array in pair])
 
 
 def body(
@@ -302,42 +326,83 @@
     padded = jnp.pad(tokens, ((0, SPARE), (0, 0)))
     gathered = lax.all_gather(padded, "replica", axis=0, tiled=False)
 
+    low = capacity // 3
+    lots = ((0, 1), (1, 1), (2, 1))
+    lot_slots = [groups * count * low for _, count in lots]
+
+    def lot_of(rows, lot):
+        first, count = lots[lot]
+        return rows[:, first * low : (first + count) * low].reshape(lot_slots[lot], -1)
+
     placing, slot_gate = routing_tables(expert_ids, gate_values, experts, capacity)
     sent_grads = (
         jnp.dot(placing, cotangent, preferred_element_type=jnp.float32) * slot_gate[:, None]
     ).astype(jnp.bfloat16)
     sent_grads = sent_grads.reshape(experts, capacity, features)
-    stored_rows = pick_stored(stored, held_at, holding, experts * capacity)
+    stored_rows = pick_stored(stored, held_at, holding, lot_slots[2])
     sent_grads, stored_rows = lax.optimization_barrier((sent_grads, stored_rows))
     arrived_grads = lax.all_to_all(sent_grads, "expert", split_axis=0, concat_axis=0, tiled=True)
-    grad_rows = arrived_grads.reshape(-1, features)
-    hidden_part = hidden_product(down_weight[0], grad_rows, stored_rows, shares)
-    hidden_part, got[4] = lax.optimization_barrier((hidden_part, got[4]))
-    hidden_grad = lax.psum_scatter(hidden_part, "replica", scatter_dimension=0, tiled=True)
+    w_down = down_weight[0]
+    early = jnp.concatenate([lot_of(arrived_grads, 0), lot_of(arrived_grads, 1)], axis=0)
+    hidden_first = hidden_product(w_down, early, None, shares)
+    hidden_first, got[4] = lax.optimization_barrier((hidden_first, got[4]))
+    hidden_second = hidden_product(w_down, lot_of(arrived_grads, 2), stored_rows, shares)
+    grads_first = lax.psum_scatter(hidden_first, "replica", scatter_dimension=0, tiled=True)
 
     behind = (here - jnp.arange(shares, dtype=jnp.int32)) % shares
     whole_tokens = jnp.take(gathered[:, :tok_rows], behind, axis=0)
     whole_tokens = whole_tokens.transpose(1, 0, 2).reshape(tok_rows, width)
     sent_rows = jnp.dot(placing, whole_tokens, preferred_element_type=jnp.float32)
     sent_rows = sent_rows.astype(jnp.bfloat16).reshape(experts, capacity, width)
-    sent_rows, got[3], got[5] = lax.optimization_barrier((sent_rows, got[3], got[5]))
+    sent_rows, hidden_second, got[1], got[7] = lax.optimization_barrier(
+        (sent_rows, hidden_second, got[1], got[7])
+    )
     arrived = lax.all_to_all(sent_rows, "expert", split_axis=0, concat_axis=0, tiled=True)
-    slot_rows = arrived.reshape(-1, width)
-    weights = [got[d] for d in range(shares)]
-
-    own, shown = hidden_gates(weights, slot_rows, hidden_grad, 2 * BLOCK)
-    partial_grad = slot_parts(own, weights, 2 * BLOCK).reshape(experts, capacity, width)
-    returned = lax.all_to_all(partial_grad, "expert", split_axis=0, concat_axis=0, tiled=True)
-
-    shown = lax.all_gather(shown, "replica", axis=0, tiled=False)
-    grad_gate = shown[:, :own_hidden].reshape(hidden, -1)
-    stored_rows = restore(
-        shown[:, own_hidden:].reshape(-1, experts * capacity), select, hidden
-    )
-
-    gradient = jnp.einsum(
-        "sd,fs->df", slot_rows[:, :features], grad_gate, preferred_element_type=jnp.float32
-    ) + stored.astype(jnp.float32)
+    hidden_second, arrived, *weights = lax.optimization_barrier(
+        (hidden_second, arrived, *[got[d] for d in range(shares)])
+    )
+    grads_second = lax.psum_scatter(hidden_second, "replica", scatter_dimension=0, tiled=True)
+
+    def give_back(parts):
+        parts = parts.reshape(experts, -1, width)
+        back = lax.all_to_all(parts, "expert", split_axis=0, concat_axis=0, tiled=True)
+        return back.reshape(-1, width)
+
+    tiles = arrived.reshape(groups, capacity // low, low, width)
+    tile = lot_slots[0]
+    own, parts, back = {}, {}, {}
+    for lot in (0, 1):
+        own[lot] = hidden_gates(weights, tiles, *lots[lot], grads_first, lot, tile)
+        parts[lot] = slot_parts(own[lot], weights, tile)
+    back[0] = give_back(parts[0])
+    grads_second, parts[1], back[0] = lax.optimization_barrier((grads_second, parts[1], back[0]))
+    back[1] = give_back(parts[1])
+    own[2] = hidden_gates(weights, tiles, *lots[2], grads_second[:own_hidden], 0, tile)
+    parts[2] = slot_parts(own[2], weights, tile)
+    parts[2], back[1] = lax.optimization_barrier((parts[2], back[1]))
+    back[2] = give_back(parts[2])
+
+    shown = jnp.concatenate(
+        [own[lot][:own_hidden] for lot in range(3)] + [grads_second[own_hidden:]], axis=1
+    )
+    shown = lax.all_gather(shown, "replica", axis=0, tiled=True)
+    slots = sum(lot_slots)
+    placed = (here - block_ids[0] // local_blocks) % shares
+    picked_at = placed * features + block_ids[0] % local_blocks * BLOCK
+    wanted = jnp.concatenate(
+        [
+            lax.dynamic_slice_in_dim(arrived, picked_at[i], BLOCK, axis=2)
+            for i in range(select)
+        ]
+        + [arrived[:, :, :features]],
+        axis=2,
+    )
+    wanted = jnp.concatenate([lot_of(wanted, lot) for lot in range(3)], axis=0)
+    wanted = jnp.pad(wanted, ((0, shown.shape[1] - slots), (0, 0)))
+    wanted, shown = lax.optimization_barrier((wanted, shown))
+    products = jnp.einsum("sd,fs->df", wanted, shown, preferred_element_type=jnp.float32)
+    block_sums = add_stored(products, shown, slots // tile, select)
+    gradient = products[select * BLOCK :] + stored.astype(jnp.float32)
     struck = jnp.any(
         local_ids[:, None] == jnp.arange(local_blocks, dtype=jnp.int32)[None, :], axis=0
     )
@@ -351,18 +416,10 @@
         .astype(jnp.bfloat16)
     )
 
-    placed = (here - block_ids[0] // local_blocks) % shares
-    picked_at = placed * features + block_ids[0] % local_blocks * BLOCK
-    picked = jnp.concatenate(
-        [
-            lax.dynamic_slice_in_dim(slot_rows, picked_at[i], BLOCK, axis=1)
-            for i in range(select)
-        ],
-        axis=1,
-    )
-    block_sums = jnp.einsum("sk,fs->kf", picked, grad_gate, preferred_element_type=jnp.float32)
-    block_sums = block_sums.reshape(select, BLOCK, hidden) + stored_rows.astype(jnp.float32)
-    combined = combine(placing.T, returned.reshape(experts * capacity, width), behind, sides)
+    placing = placing.reshape(experts, capacity, tok_rows)
+    combined = combine(
+        [(lot_of(placing, lot).T, back[lot]) for lot in range(3)], behind, sides
+    )
     combined = combined.reshape(sides * shares, tok_rows // sides, features)
     collected = lax.all_to_all(
         combined, ("tensor", "replica"), split_axis=0, concat_axis=0, tiled=True

time: 322 us -> 312 us (0.969)
  waiting for transfers between devices: 187 us -> 146 us
  Pallas kernels: 33.1 us -> 52.1 us
  starting transfers between devices: 49.8 us -> 59.2 us
  other arithmetic: 3.65 us -> 7.84 us
    ppermute x7, waiting for transfers between devices: 106 us -> 85.7 us  [hand_out(): return lax.ppermute(pieces[d], 'replica', shift_by(d, shares))]
    all_to_all x1 -> x3, waiting for transfers between devices: 58.8 us -> 39.3 us  [give_back(): lax.all_to_all(parts, 'expert', split_axis=0, concat_axis=0, tiled=True)]
    all_to_all x1 -> x3, starting transfers between devices: 5.5 us -> 16.6 us  [give_back(): lax.all_to_all(parts, 'expert', split_axis=0, concat_axis=0, tiled=True)]
    pallas_call x1 -> x3, Pallas kernels: 8.58 us -> 15.3 us  [hidden_gates(): pl.pallas_call(gates_kernel, grid=(slots // tile,), in_specs=[pl.BlockSpe...]
    pallas_call x1 -> x3, Pallas kernels: 9 us -> 15.7 us  [slot_parts(): pl.pallas_call(part_kernel, grid=(slots // tile,), in_specs=[pl.BlockSpec...]
    pallas_call x1 -> x2, Pallas kernels: 3.7 us -> 9.19 us  [hidden_product(): pl.pallas_call(hidden_kernel, grid=(steps,), in_specs=[pl.BlockSpec((high...]
    unnamed x40 -> x36, local copies, waits for them, and re-layouts: 6.85 us -> 2.99 us
    slice x5 -> x11, local copies, waits for them, and re-layouts: 2.17 us -> 5.93 us  [the longest x3 1.96 us: lot_of(): rows[:, first * low:(first + count) * low].reshape(lot_slots[lot], -1)]
  transfers between devices with their start and end apart: 14 -> 17, of which waited for: 10 -> 13; matrix products, arithmetic and copies ran while one was open for 7% -> 8% of each run, Pallas kernels for 8% -> 15%
where the time goes in v2:
time: 312 us; the launch traced here: 311 us
  waiting for transfers between devices  146 us (47%)
  starting transfers between devices  59.2 us (19%)
  Pallas kernels  52.1 us (17%)
  between operations  18 us (6%)
  local copies, waits for them, and re-layouts  15.6 us (5%)
  matrix products  11.7 us (4%)
  other arithmetic  7.84 us (3%)
    ppermute x7, waiting for transfers between devices, hand_out(): return lax.ppermute(pieces[d], 'replica', shift_by(d, shares))  85.7 us
    all_to_all x3, waiting for transfers between devices, give_back(): lax.all_to_all(parts, 'expert', split_axis=0, concat_axis=0, tiled=True)  39.3 us
    ppermute x7, starting transfers between devices, hand_out(): return lax.ppermute(pieces[d], 'replica', shift_by(d, shares))  23.5 us
    all_to_all x3, starting transfers between devices, give_back(): lax.all_to_all(parts, 'expert', split_axis=0, concat_axis=0, tiled=True)  16.6 us
    pallas_call x3, Pallas kernels, slot_parts(): pl.pallas_call(part_kernel, grid=(slots // tile,), in_specs=[pl.BlockSpec...  15.7 us
    pallas_call x3, Pallas kernels, hidden_gates(): pl.pallas_call(gates_kernel, grid=(slots // tile,), in_specs=[pl.BlockSpe...  15.3 us
    all_to_all x1, waiting for transfers between devices, body(): lax.all_to_all(combined, ('tensor', 'replica'), split_axis=0, concat_axis...  9.4 us
    pallas_call x2, Pallas kernels, hidden_product(): pl.pallas_call(hidden_kernel, grid=(steps,), in_specs=[pl.BlockSpec((high...  9.19 us
  transfers between devices with their start and end apart: 17, of which 13 were waited for; matrix products, arithmetic and copies ran while one was open for 8% of the time, Pallas kernels for 15%

profile of v2, /device:TPU:8, one launch (start us, length us, event | category | flops | bytes accessed | tf_op | source)
XLA Modules:
  0.0 310.8 jit_solution(10411251582827606116)
XLA Ops:
  7.2 1.6 pad.8
  8.8 6.9 %shard_map.112 = (bf16[672,384]{1,0:T(8,128)(2,1)}, bf16[672,384]{1,0:T(8,128)(2,1)}, bf16[672,384]{1,0:T(8,128)(2,1)}, bf16[672,384]{1,0:T(8,128)(2,1)}, bf16[6...) custom-call(s32[1]{0:T(128)} %bitcast.refs_0_, ...), custom_call_target="tpu_custom_call" | custom-call | bytes 8257536 | tf_op jit(solution)/shard_map/pallas_call | solution.py:53
  16.0 1.2 reduce-window.6
  18.8 0.9 select_reduce_fusion
  19.7 1.1 fusion.6
  20.9 6.2 %all-to-all-start = ((bf16[16,48,384]{2,1,0:T(8,128)(2,1)}), bf16[16,48,384]{2,1,0:T(8,128)(2,1)}, u32[]{:S(2)}, u32[]{:S(2)}) async-start(bf16[16,48,384]{2,1,0:T(8,128)(2,1)} %bitcast.100), calls=%async_computation | async-start | bytes 1179648 | tf_op jit(solution)/shard_map/all_to_all | solution.py:344
  27.1 6.9 %collective-permute-start.4 = (bf16[672,384]{1,0:T(8,128)(2,1)}, bf16[672,384]{1,0:T(8,128)(2,1)}, u32[]{:S(2)}, u32[]{:S(2)}) collective-permute-start(bf16[672,384]{1,0:T(8,128)(2,1)} %get-tuple-element.67), channel_id=1, source_target_pairs={{0,4},{1,5},{2,6},{3,7},{4,0},{5,1},{6,2},{7,3},{8,12},{9,13},{10,... | collective-permute-start | bytes 1548296 | tf_op jit(solution)/shard_map/ppermute | solution.py:322
  34.0 3.2 %all-to-all-done = bf16[16,48,384]{2,1,0:T(8,128)(2,1)} async-done(((bf16[16,48,384]{2,1,0:T(8,128)(2,1)}), bf16[16,48,384]{2,1,0:T(8,128)(2,1)}, u32[]{:S(2)}, u32[]{:S(2)}) %all-to-all-start) | async-done | bytes 589856 | tf_op jit(solution)/shard_map/all_to_all | solution.py:344
  37.2 1.9 fusion.22
  39.1 4.8 %shard_map.115 = bf16[2688,512]{1,0:T(8,128)(2,1)} custom-call(bf16[2688,384]{1,0:T(8,128)(2,1)S(1)} %bitcast.84, bf16[512,384]{1,0:T(8,128)(2,1)S(1)} %pad_maximum_fusion.2.rows_ref), custom_call_target="tpu_custom_call" | custom-call | flops 1056964608 | bytes 7962624 | tf_op jit(solution)/shard_map/pallas_call | solution.py:156
  43.9 14.5 %collective-permute-done.4.refs_4_ = bf16[672,384]{1,0:T(8,128)(2,1)} collective-permute-done((bf16[672,384]{1,0:T(8,128)(2,1)}, bf16[672,384]{1,0:T(8,128)(2,1)}, u32[]{:S(2)}, u32[]{:S(2)}) %collective-permute-start.4) | collective-permute-done | bytes 516128 | tf_op jit(solution)/shard_map/ppermute | solution.py:322
  58.4 7.1 %collective-permute-start = (bf16[672,384]{1,0:T(8,128)(2,1)}, bf16[672,384]{1,0:T(8,128)(2,1)}, u32[]{:S(2)}, u32[]{:S(2)}) collective-permute-start(bf16[672,384]{1,0:T(8,128)(2,1)} %get-tuple-element.59), channel_id=1, source_target_pairs={{0,1},{1,2},{2,3},{3,4},{4,5},{5,6},{6,7},{7,0},{8,9},{9,10},{10,1... | collective-permute-start | bytes 1548296 | tf_op jit(solution)/shard_map/ppermute | solution.py:322
  66.7 4.4 %shard_map.114 = bf16[5376,256]{1,0:T(8,128)(2,1)} custom-call(bf16[2688,384]{1,0:T(8,128)(2,1)S(1)} %bitcast.85, bf16[256,384]{1,0:T(8,128)(2,1)S(1)} %bitcast.90, bf16[2688,256]{1,0:T(8,128)(2,1)S(1)} %shard_map.113.refs_0_), custom_call_target="tpu_custom_call" | custom-call | flops 528482304 | bytes 7766016 | tf_op jit(solution)/shard_map/pallas_call | solution.py:156
  71.1 1.2 slice.88
  74.0 3.5 %convolution_convert_fusion = bf16[768,3072]{1,0:T(8,128)(2,1)} fusion(pred[768,128]{1,0:T(8,128)(4,1)S(1)} %copy-done.13, bf16[128,3072]{0,1:T(8,128)(2,1)S(1)} %bitcast.98), kind=kOutput, calls=%fused_computation.1 | convolution fusion | flops 606339072 | bytes 5603328 | tf_op jit(solution)/shard_map/dot_general | solution.py:355
  77.7 1.3 collective-permute-done.1.refs_7_
  79.0 5.8 %all-to-all-start.1 = ((bf16[16,48,3072]{2,1,0:T(8,128)(2,1)}), bf16[16,48,3072]{2,1,0:T(8,128)(2,1)}, u32[]{:S(2)}, u32[]{:S(2)}) async-start(bf16[16,48,3072]{2,1,0:T(8,128)(2,1)} %bitcast.94), calls=%async_computation.1 | async-start | bytes 9437184 | tf_op jit(solution)/shard_map/all_to_all | solution.py:360
  84.9 1.1 collective-permute-start.2
  86.0 4.4 %collective-permute-start.3 = (bf16[672,384]{1,0:T(8,128)(2,1)}, bf16[672,384]{1,0:T(8,128)(2,1)S(1)}, u32[]{:S(2)}, u32[]{:S(2)}) collective-permute-start(bf16[672,384]{1,0:T(8,128)(2,1)} %get-tuple-element.66), channel_id=1, source_target_pairs={{0,3},{1,4},{2,5},{3,6},{4,7},{5,0},{6,1},{7,2},{8,11},{9,12},{10,... | collective-permute-start | bytes 1548296 | tf_op jit(solution)/shard_map/ppermute | solution.py:322
  91.0 3.1 %collective-permute-start.6 = (bf16[672,384]{1,0:T(8,128)(2,1)S(1)}, bf16[672,384]{1,0:T(8,128)(2,1)S(1)}, u32[]{:S(2)}, u32[]{:S(2)}) collective-permute-start(bf16[672,384]{1,0:T(8,128)(2,1)S(1)} %copy-done.16), channel_id=1, source_target_pairs={{0,6},{1,7},{2,0},{3,1},{4,2},{5,3},{6,4},{7,5},{8,14},{9,15},{10,... | collective-permute-start | bytes 1548296 | tf_op jit(solution)/shard_map/ppermute | solution.py:322
  94.1 30.0 %collective-permute-done.2.refs_2_ = bf16[672,384]{1,0:T(8,128)(2,1)S(1)} collective-permute-done((bf16[672,384]{1,0:T(8,128)(2,1)}, bf16[672,384]{1,0:T(8,128)(2,1)S(1)}, u32[]{:S(2)}, u32[]{:S(2)}) %collective-permute-start.2) | collective-permute-done | bytes 516128 | tf_op jit(solution)/shard_map/ppermute | solution.py:322
  124.2 38.4 %collective-permute-done.3.refs_3_ = bf16[672,384]{1,0:T(8,128)(2,1)S(1)} collective-permute-done((bf16[672,384]{1,0:T(8,128)(2,1)}, bf16[672,384]{1,0:T(8,128)(2,1)S(1)}, u32[]{:S(2)}, u32[]{:S(2)}) %collective-permute-start.3) | collective-permute-done | bytes 516128 | tf_op jit(solution)/shard_map/ppermute | solution.py:322
  162.6 1.4 collective-permute-done.6.refs_6_
  164.7 5.0 %shard_map.118.own_ref = bf16[672,256]{1,0:T(8,128)(2,1)} custom-call(bf16[16,3,16,3072]{3,2,1,0:T(8,128)(2,1)} %bitcast.19.rows_ref, bf16[336,512]{1,0:T(8,128)(2,1)} %reduce-scatter.5.cloned.1.call-done.grad_ref, bf16[672,384]{1,0:T(8,128)(2,1)} %get-tuple-element.75.refs_0_, bf16[672,384]{1,0:T(8,128)(2,1)} %collective-permute-done.refs_1_, ...), custom_call_target="tpu_custom_call" | custom-call | flops 1056964608 | bytes 6389760 | tf_op jit(solution)/shard_map/pallas_call | solution.py:203
  169.8 5.2 %shard_map.119 = bf16[256,3072]{1,0:T(8,128)(2,1)} custom-call(bf16[672,256]{1,0:T(8,128)(2,1)} %shard_map.118.own_ref, bf16[672,384]{1,0:T(8,128)(2,1)} %get-tuple-element.75.refs_0_, bf16[672,384]{1,0:T(8,128)(2,1)} %collective-permute-done.refs_1_, bf16[672,384]{1,0:T(8,128)(2,1)} %copy-done.8, bf16[672,384]{1,0:T(8,128)(2,1)} %copy-done.9, ...), custom_call_target="tpu_custom_call" | custom-call | flops 1056964608 | bytes 6045696 | tf_op jit(solution)/shard_map/pallas_call | solution.py:236
  175.0 5.8 %all-to-all-start.2 = ((bf16[16,16,3072]{2,1,0:T(8,128)(2,1)}), bf16[16,16,3072]{2,1,0:T(8,128)(2,1)S(1)}, u32[]{:S(2)}, u32[]{:S(2)}) async-start(bf16[16,16,3072]{2,1,0:T(8,128)(2,1)} %bitcast.97), calls=%async_computation.4 | async-start | bytes 3145728 | tf_op jit(solution)/shard_map/all_to_all | solution.py:368
  180.8 5.1 %shard_map.116.own_ref = bf16[672,256]{1,0:T(8,128)(2,1)} custom-call(bf16[16,3,16,3072]{3,2,1,0:T(8,128)(2,1)} %bitcast.19.rows_ref, bf16[336,512]{1,0:T(8,128)(2,1)} %reduce-scatter.5.cloned.1.call-done.grad_ref, bf16[672,384]{1,0:T(8,128)(2,1)} %get-tuple-element.75.refs_0_, bf16[672,384]{1,0:T(8,128)(2,1)} %collective-permute-done.refs_1_, ...), custom_call_target="tpu_custom_call" | custom-call | flops 1056964608 | bytes 6389760 | tf_op jit(solution)/shard_map/pallas_call | solution.py:203
  185.9 5.3 %shard_map.117 = bf16[256,3072]{1,0:T(8,128)(2,1)} custom-call(bf16[672,256]{1,0:T(8,128)(2,1)} %shard_map.116.own_ref, bf16[672,384]{1,0:T(8,128)(2,1)} %get-tuple-element.75.refs_0_, bf16[672,384]{1,0:T(8,128)(2,1)} %collective-permute-done.refs_1_, bf16[672,384]{1,0:T(8,128)(2,1)} %copy-done.8, bf16[672,384]{1,0:T(8,128)(2,1)} %copy-done.9, ...), custom_call_target="tpu_custom_call" | custom-call | flops 1056964608 | bytes 6045696 | tf_op jit(solution)/shard_map/pallas_call | solution.py:236
  191.2 10.8 %all-to-all-done.2 = bf16[16,16,3072]{2,1,0:T(8,128)(2,1)S(1)} async-done(((bf16[16,16,3072]{2,1,0:T(8,128)(2,1)}), bf16[16,16,3072]{2,1,0:T(8,128)(2,1)S(1)}, u32[]{:S(2)}, u32[]{:S(2)}) %all-to-all-start.2) | async-done | bytes 1572896 | tf_op jit(solution)/shard_map/all_to_all | solution.py:368
  202.0 5.6 %reduce-scatter.3.cloned.1.call-done = bf16[672,256]{1,0:T(8,128)(2,1)} async-done(((bf16[5376,256]{1,0:T(8,128)(2,1)}), bf16[672,256]{1,0:T(8,128)(2,1)}) %reduce-scatter.3.cloned.1.call-update) | async-done | bytes 344080 | tf_op jit(solution)/shard_map/reduce_scatter | solution.py:364
  207.6 1.7 fusion.23
  209.3 5.1 %shard_map.120.own_ref = bf16[672,256]{1,0:T(8,128)(2,1)} custom-call(bf16[16,3,16,3072]{3,2,1,0:T(8,128)(2,1)} %bitcast.19.rows_ref, bf16[336,256]{1,0:T(8,128)(2,1)} %get-tuple-element.104.grad_ref, bf16[672,384]{1,0:T(8,128)(2,1)} %get-tuple-element.75.refs_0_, bf16[672,384]{1,0:T(8,128)(2,1)} %collective-permute-done.refs_1_, ...), custom_call_target="tpu_custom_call" | custom-call | flops 1056964608 | bytes 6389760 | tf_op jit(solution)/shard_map/pallas_call | solution.py:203
  215.4 0.9 pad_maximum_fusion.1
  216.4 5.7 %all-to-all-start.3 = ((bf16[16,16,3072]{2,1,0:T(8,128)(2,1)}), bf16[16,16,3072]{2,1,0:T(8,128)(2,1)S(1)}, u32[]{:S(2)}, u32[]{:S(2)}) async-start(bf16[16,16,3072]{2,1,0:T(8,128)(2,1)} %bitcast.96), calls=%async_computation.5 | async-start | bytes 3145728 | tf_op jit(solution)/shard_map/all_to_all | solution.py:368
  222.1 5.2 %shard_map.121 = bf16[256,3072]{1,0:T(8,128)(2,1)} custom-call(bf16[672,256]{1,0:T(8,128)(2,1)} %shard_map.120.own_ref, bf16[672,384]{1,0:T(8,128)(2,1)} %get-tuple-element.75.refs_0_, bf16[672,384]{1,0:T(8,128)(2,1)} %collective-permute-done.refs_1_, bf16[672,384]{1,0:T(8,128)(2,1)} %copy-done.8, bf16[672,384]{1,0:T(8,128)(2,1)} %copy-done.9, ...), custom_call_target="tpu_custom_call" | custom-call | flops 1056964608 | bytes 6045696 | tf_op jit(solution)/shard_map/pallas_call | solution.py:236
  227.3 16.0 %all-to-all-done.3 = bf16[16,16,3072]{2,1,0:T(8,128)(2,1)S(1)} async-done(((bf16[16,16,3072]{2,1,0:T(8,128)(2,1)}), bf16[16,16,3072]{2,1,0:T(8,128)(2,1)S(1)}, u32[]{:S(2)}, u32[]{:S(2)}) %all-to-all-start.3) | async-done | bytes 1572896 | tf_op jit(solution)/shard_map/all_to_all | solution.py:368
  243.3 5.2 %all-to-all-start.4 = ((bf16[16,16,3072]{2,1,0:T(8,128)(2,1)}), bf16[16,16,3072]{2,1,0:T(8,128)(2,1)}, u32[]{:S(2)}, u32[]{:S(2)}) async-start(bf16[16,16,3072]{2,1,0:T(8,128)(2,1)} %bitcast.95), calls=%async_computation.6 | async-start | bytes 3145728 | tf_op jit(solution)/shard_map/all_to_all | solution.py:368
  253.5 1.1 slice.75
  254.7 1.3 constant_dynamic-slice_fusion.1
  256.2 1.2 fusion.8
  257.4 12.5 %all-to-all-done.4 = bf16[16,16,3072]{2,1,0:T(8,128)(2,1)} async-done(((bf16[16,16,3072]{2,1,0:T(8,128)(2,1)}), bf16[16,16,3072]{2,1,0:T(8,128)(2,1)}, u32[]{:S(2)}, u32[]{:S(2)}) %all-to-all-start.4) | async-done | bytes 1572896 | tf_op jit(solution)/shard_map/all_to_all | solution.py:368
  269.8 2.4 shard_map.122
  273.2 6.9 %all-to-all-start.5 = ((bf16[16,64,384]{2,1,0:T(8,128)(2,1)}), bf16[16,64,384]{2,1,0:T(8,128)(2,1)S(1)}, u32[]{:S(2)}, u32[]{:S(2)}) async-start(bf16[16,64,384]{2,1,0:T(8,128)(2,1)} %bitcast.89), calls=%async_computation.7 | async-start | bytes 1572864 | tf_op jit(solution)/shard_map/all_to_all | solution.py:424
  280.0 3.0 all-gather.4.cloned.1.call-done.packed_ref
  283.1 7.0 %fusion.26.products_ref = f32[640,2688]{1,0:T(8,128)S(1)} fusion(bf16[1024,640]{1,0:T(8,128)(2,1)} %fusion.8, bf16[2688,1024]{1,0:T(8,128)(2,1)} %all-gather.4.cloned.1.call-done.packed_ref), kind=kOutput, calls=%fused_computation.65 | convolution fusion | flops 3523215360 | bytes 13697024 | tf_op jit(solution)/shard_map/sd,fs->df/dot_general | solution.py:403
  290.1 2.0 shard_map.123
  292.1 2.0 fusion.1
  294.2 9.4 %all-to-all-done.5 = bf16[16,64,384]{2,1,0:T(8,128)(2,1)S(1)} async-done(((bf16[16,64,384]{2,1,0:T(8,128)(2,1)}), bf16[16,64,384]{2,1,0:T(8,128)(2,1)S(1)}, u32[]{:S(2)}, u32[]{:S(2)}) %all-to-all-start.5) | async-done | bytes 786464 | tf_op jit(solution)/shard_map/all_to_all | solution.py:424
  (90 shorter events, 10.5 us)
Async XLA Ops:
  7.2 12.6 %copy-start = (bf16[128,384]{1,0:T(8,128)(2,1)S(1)}, bf16[128,384]{1,0:T(8,128)(2,1)}, u32[]{:S(2)}) copy-start(bf16[128,384]{1,0:T(8,128)(2,1)} %param.10) | copy-start | bytes 294916
  7.2 63.9 %all-gather.6.cloned.1.call-start = ((), (), s32[]{:S(2)}) async-start(), calls=%async_computation.11 | async-start | bytes 1216512 | tf_op jit(solution)/shard_map/all_gather | solution.py:327
  8.8 6.9 %copy-start.14 = (s32[128,4]{0,1:T(4,128)S(1)}, s32[128,4]{0,1:T(4,128)}, u32[]{:S(2)}) copy-start(s32[128,4]{0,1:T(4,128)} %param.12) | copy-start | bytes 6148
  8.8 8.9 %copy-start.15 = (s32[1,2]{1,0:T(1,128)S(1)}, s32[1,2]{1,0:T(1,128)}, u32[]{:S(2)}) copy-start(s32[1,2]{1,0:T(1,128)} %param.16) | copy-start | bytes 28
  8.8 9.0 %copy-start.3 = (bf16[1,384,2688]{2,1,0:T(8,128)(2,1)S(1)}, bf16[1,384,2688]{2,1,0:T(8,128)(2,1)}, u32[]{:S(2)}) copy-start(bf16[1,384,2688]{2,1,0:T(8,128)(2,1)} %param.17) | copy-start | bytes 6193156
  18.8 1.0 copy-start.12
  19.7 19.4 %copy-start.2 = (bf16[1,2688,384]{2,1,0:T(8,128)(2,1)S(1)}, bf16[1,2688,384]{2,1,0:T(8,128)(2,1)}, u32[]{:S(2)}) copy-start(bf16[1,2688,384]{2,1,0:T(8,128)(2,1)} %param.15) | copy-start | bytes 6193156
  20.9 16.3 %all-to-all-start = ((bf16[16,48,384]{2,1,0:T(8,128)(2,1)}), bf16[16,48,384]{2,1,0:T(8,128)(2,1)}, u32[]{:S(2)}, u32[]{:S(2)}) async-start(bf16[16,48,384]{2,1,0:T(8,128)(2,1)} %bitcast.100), calls=%async_computation | async-start | bytes 1179648 | tf_op jit(solution)/shard_map/all_to_all | solution.py:344
  27.1 136.9 %reduce-scatter.5.cloned.1.call-start = ((), (), s32[]{:S(2)}) async-start(), calls=%async_computation.9 | async-start | bytes 3096576 | tf_op jit(solution)/shard_map/reduce_scatter | solution.py:350
  27.1 31.3 %collective-permute-start.4 = (bf16[672,384]{1,0:T(8,128)(2,1)}, bf16[672,384]{1,0:T(8,128)(2,1)}, u32[]{:S(2)}, u32[]{:S(2)}) collective-permute-start(bf16[672,384]{1,0:T(8,128)(2,1)} %get-tuple-element.67), channel_id=1, source_target_pairs={{0,4},{1,5},{2,6},{3,7},{4,0},{5,1},{6,2},{7,3},{8,12},{9,13},{10,... | collective-permute-start | bytes 1548296 | tf_op jit(solution)/shard_map/ppermute | solution.py:322
  58.4 19.2 %collective-permute-start = (bf16[672,384]{1,0:T(8,128)(2,1)}, bf16[672,384]{1,0:T(8,128)(2,1)}, u32[]{:S(2)}, u32[]{:S(2)}) collective-permute-start(bf16[672,384]{1,0:T(8,128)(2,1)} %get-tuple-element.59), channel_id=1, source_target_pairs={{0,1},{1,2},{2,3},{3,4},{4,5},{5,6},{6,7},{7,0},{8,9},{9,10},{10,1... | collective-permute-start | bytes 1548296 | tf_op jit(solution)/shard_map/ppermute | solution.py:322
  65.5 13.5 %collective-permute-start.1 = (bf16[672,384]{1,0:T(8,128)(2,1)}, bf16[672,384]{1,0:T(8,128)(2,1)}, u32[]{:S(2)}, u32[]{:S(2)}) collective-permute-start(bf16[672,384]{1,0:T(8,128)(2,1)} %get-tuple-element.60), channel_id=1, source_target_pairs={{0,7},{1,0},{2,1},{3,2},{4,3},{5,4},{6,5},{7,6},{8,15},{9,8},{10,9... | collective-permute-start | bytes 1548296 | tf_op jit(solution)/shard_map/ppermute | solution.py:322
  65.8 0.9 copy-start.7
  73.1 0.9 copy-start.13
  79.0 11.4 %copy-start.17 = (bf16[672,384]{1,0:T(8,128)(2,1)S(1)}, bf16[672,384]{1,0:T(8,128)(2,1)}, u32[]{:S(2)}) copy-start(bf16[672,384]{1,0:T(8,128)(2,1)} %get-tuple-element.69) | copy-start | bytes 1548292
  79.0 12.0 %copy-start.16 = (bf16[672,384]{1,0:T(8,128)(2,1)S(1)}, bf16[672,384]{1,0:T(8,128)(2,1)}, u32[]{:S(2)}) copy-start(bf16[672,384]{1,0:T(8,128)(2,1)} %get-tuple-element.70) | copy-start | bytes 1548292
  79.0 85.0 %all-to-all-start.1 = ((bf16[16,48,3072]{2,1,0:T(8,128)(2,1)}), bf16[16,48,3072]{2,1,0:T(8,128)(2,1)}, u32[]{:S(2)}, u32[]{:S(2)}) async-start(bf16[16,48,3072]{2,1,0:T(8,128)(2,1)} %bitcast.94), calls=%async_computation.1 | async-start | bytes 9437184 | tf_op jit(solution)/shard_map/all_to_all | solution.py:360
  84.8 122.8 %reduce-scatter.3.cloned.1.call-start = ((), (), s32[]{:S(2)}) async-start(), calls=%async_computation.8 | async-start | bytes 3096576 | tf_op jit(solution)/shard_map/reduce_scatter | solution.py:364
  84.9 39.3 %collective-permute-start.2 = (bf16[672,384]{1,0:T(8,128)(2,1)}, bf16[672,384]{1,0:T(8,128)(2,1)S(1)}, u32[]{:S(2)}, u32[]{:S(2)}) collective-permute-start(bf16[672,384]{1,0:T(8,128)(2,1)} %get-tuple-element.65), channel_id=1, source_target_pairs={{0,2},{1,3},{2,4},{3,5},{4,6},{5,7},{6,0},{7,1},{8,10},{9,11},{10,... | collective-permute-start | bytes 1548296 | tf_op jit(solution)/shard_map/ppermute | solution.py:322
  86.0 76.6 %collective-permute-start.3 = (bf16[672,384]{1,0:T(8,128)(2,1)}, bf16[672,384]{1,0:T(8,128)(2,1)S(1)}, u32[]{:S(2)}, u32[]{:S(2)}) collective-permute-start(bf16[672,384]{1,0:T(8,128)(2,1)} %get-tuple-element.66), channel_id=1, source_target_pairs={{0,3},{1,4},{2,5},{3,6},{4,7},{5,0},{6,1},{7,2},{8,11},{9,12},{10,... | collective-permute-start | bytes 1548296 | tf_op jit(solution)/shard_map/ppermute | solution.py:322
  90.4 72.2 %collective-permute-start.5 = (bf16[672,384]{1,0:T(8,128)(2,1)S(1)}, bf16[672,384]{1,0:T(8,128)(2,1)S(1)}, u32[]{:S(2)}, u32[]{:S(2)}) collective-permute-start(bf16[672,384]{1,0:T(8,128)(2,1)S(1)} %copy-done.17), channel_id=1, source_target_pairs={{0,5},{1,6},{2,7},{3,0},{4,1},{5,2},{6,3},{7,4},{8,13},{9,14},{10,... | collective-permute-start | bytes 1548296 | tf_op jit(solution)/shard_map/ppermute | solution.py:322
  91.0 72.9 %collective-permute-start.6 = (bf16[672,384]{1,0:T(8,128)(2,1)S(1)}, bf16[672,384]{1,0:T(8,128)(2,1)S(1)}, u32[]{:S(2)}, u32[]{:S(2)}) collective-permute-start(bf16[672,384]{1,0:T(8,128)(2,1)S(1)} %copy-done.16), channel_id=1, source_target_pairs={{0,6},{1,7},{2,0},{3,1},{4,2},{5,3},{6,4},{7,5},{8,14},{9,15},{10,... | collective-permute-start | bytes 1548296 | tf_op jit(solution)/shard_map/ppermute | solution.py:322
  124.2 39.8 %copy-start.8 = (bf16[672,384]{1,0:T(8,128)(2,1)}, bf16[672,384]{1,0:T(8,128)(2,1)S(1)}, u32[]{:S(2)}) copy-start(bf16[672,384]{1,0:T(8,128)(2,1)S(1)} %collective-permute-done.2.refs_2_) | copy-start | bytes 1548292
  162.6 1.4 copy-start.9
  162.6 1.4 copy-start.10
  163.9 0.8 copy-start.11
  175.0 27.0 %all-to-all-start.2 = ((bf16[16,16,3072]{2,1,0:T(8,128)(2,1)}), bf16[16,16,3072]{2,1,0:T(8,128)(2,1)S(1)}, u32[]{:S(2)}, u32[]{:S(2)}) async-start(bf16[16,16,3072]{2,1,0:T(8,128)(2,1)} %bitcast.97), calls=%async_computation.4 | async-start | bytes 3145728 | tf_op jit(solution)/shard_map/all_to_all | solution.py:368
  180.7 102.3 %all-gather.4.cloned.1.call-start = ((), (), s32[]{:S(2)}) async-start(), calls=%async_computation.10 | async-start | bytes 6193152 | tf_op jit(solution)/shard_map/all_gather | solution.py:388
  209.3 6.1 %slice-start = ((bf16[672,256]{1,0:T(8,128)(2,1)}), bf16[336,256]{1,0:T(8,128)(2,1)S(1)}, s32[]{:S(2)}) async-start(bf16[672,256]{1,0:T(8,128)(2,1)} %shard_map.118.own_ref), calls=%async_computation.12 | async-start | bytes 344064 | tf_op jit(solution)/shard_map/slice | solution.py:386
  209.3 6.1 %slice-start.1 = ((bf16[672,256]{1,0:T(8,128)(2,1)}), bf16[336,256]{1,0:T(8,128)(2,1)S(1)}, s32[]{:S(2)}) async-start(bf16[672,256]{1,0:T(8,128)(2,1)} %shard_map.116.own_ref), calls=%async_computation.13 | async-start | bytes 344064 | tf_op jit(solution)/shard_map/slice | solution.py:386
  216.4 27.0 %all-to-all-start.3 = ((bf16[16,16,3072]{2,1,0:T(8,128)(2,1)}), bf16[16,16,3072]{2,1,0:T(8,128)(2,1)S(1)}, u32[]{:S(2)}, u32[]{:S(2)}) async-start(bf16[16,16,3072]{2,1,0:T(8,128)(2,1)} %bitcast.96), calls=%async_computation.5 | async-start | bytes 3145728 | tf_op jit(solution)/shard_map/all_to_all | solution.py:368
  243.3 26.5 %all-to-all-start.4 = ((bf16[16,16,3072]{2,1,0:T(8,128)(2,1)}), bf16[16,16,3072]{2,1,0:T(8,128)(2,1)}, u32[]{:S(2)}, u32[]{:S(2)}) async-start(bf16[16,16,3072]{2,1,0:T(8,128)(2,1)} %bitcast.95), calls=%async_computation.6 | async-start | bytes 3145728 | tf_op jit(solution)/shard_map/all_to_all | solution.py:368
  272.3 0.9 copy-start.6
  273.2 30.4 %all-to-all-start.5 = ((bf16[16,64,384]{2,1,0:T(8,128)(2,1)}), bf16[16,64,384]{2,1,0:T(8,128)(2,1)S(1)}, u32[]{:S(2)}, u32[]{:S(2)}) async-start(bf16[16,64,384]{2,1,0:T(8,128)(2,1)} %bitcast.89), calls=%async_computation.7 | async-start | bytes 1572864 | tf_op jit(solution)/shard_map/all_to_all | solution.py:424
  283.1 7.0 %copy-start.5 = (bf16[2688,1024]{1,0:T(8,128)(2,1)S(1)}, bf16[2688,1024]{1,0:T(8,128)(2,1)}, u32[]{:S(2)}) copy-start(bf16[2688,1024]{1,0:T(8,128)(2,1)} %all-gather.4.cloned.1.call-done.packed_ref) | copy-start | bytes 16515076
  290.1 2.0 copy-start.4
  292.1 12.2 %copy-start.1 = (bf16[128,384]{1,0:T(8,128)(2,1)S(1)}, bf16[128,384]{1,0:T(8,128)(2,1)}, u32[]{:S(2)}) copy-start(bf16[128,384]{1,0:T(8,128)(2,1)} %param.10) | copy-start | bytes 294916
Sparse Core Ops, SparseCore 0:
  9.8 51.4 all-gather.5
  64.5 89.4 reduce-scatter.4
  164.1 43.4 reduce-scatter.2
  216.5 66.5 all-gather.3

commit v3 on v2

--- a/solution.py
+++ b/solution.py
@@ -172,10 +172,10 @@
     )(weight, rows, *more)
 
 
-def gates_kernel(rows_ref, grad_ref, *refs):
-    weights, own_ref = refs[:-1], refs[-1]
-    own_hidden, depth = own_ref.shape[0] // 2, weights[0].shape[1]
-    slots = own_ref.shape[1]
+def gates_kernel(shares, rows_ref, grad_ref, *refs):
+    weights, others = refs[:shares], refs[shares:]
+    own_hidden, depth = grad_ref.shape[0], weights[0].shape[1]
+    slots = grad_ref.shape[1]
     pre = None
     for d, weight in enumerate(weights):
         term = lax.dot_general(
@@ -188,57 +188,82 @@
     gate_pre, up_pre = pre[:own_hidden], pre[own_hidden:]
     hidden_grad = grad_ref[...].astype(jnp.float32)
     squashed = 1.0 / (1.0 + jnp.exp(-gate_pre))
-    own_ref[:own_hidden, :] = (
-        hidden_grad * up_pre * squashed * (1.0 + gate_pre * (1.0 - squashed))
-    ).astype(own_ref.dtype)
-    own_ref[own_hidden:, :] = (hidden_grad * gate_pre * squashed).astype(own_ref.dtype)
-
-
-def hidden_gates(weights, rows, first, count, hidden_grad, at, tile):
+    grad_gate = (hidden_grad * up_pre * squashed * (1.0 + gate_pre * (1.0 - squashed))).astype(
+        jnp.bfloat16
+    )
+    grad_up = (hidden_grad * gate_pre * squashed).astype(jnp.bfloat16)
+    own_ref = others[-1]
+    at = own_ref.shape[1] - slots
+    own_ref[:own_hidden, at:] = grad_gate
+    own_ref[own_hidden:, at:] = grad_up
+    if len(others) > 1:
+        first_ref, second_ref, extra_ref, shown_ref, _ = others
+        own_ref[:, :at] = second_ref[...]
+        for lot, rows in enumerate(
+            (first_ref[...], second_ref[:own_hidden, :], grad_gate, extra_ref[...])
+        ):
+            shown_ref[:, lot * slots : (lot + 1) * slots] = rows
+
+
+def hidden_gates(weights, rows, lot, hidden_grad, at, earlier=()):
     groups, _, low, width = rows.shape
-    high, slots = weights[0].shape[0], groups * count * low
+    high, slots = weights[0].shape[0], groups * low
     own_hidden = high // 2
-    block = (tile // (count * low), count, low, width)
-    whole = pl.BlockSpec(weights[0].shape, lambda i: (0, 0))
-    return pl.pallas_call(
-        gates_kernel,
-        grid=(slots // tile,),
-        in_specs=[
-            pl.BlockSpec(block, lambda i: (i, first // count, 0, 0)),
-            pl.BlockSpec((own_hidden, tile), lambda i: (0, at + i)),
+    wide = 2 * slots if earlier else slots
+    out_shape = [jax.ShapeDtypeStruct((high, wide), jnp.bfloat16)]
+    in_specs = [
+        pl.BlockSpec((groups, 1, low, width), lambda i: (0, lot, 0, 0)),
+        pl.BlockSpec((own_hidden, slots), lambda i: (0, at)),
+    ] + [pl.BlockSpec(weights[0].shape, lambda i: (0, 0))] * len(weights)
+    operands = [rows, hidden_grad, *weights]
+    if earlier:
+        in_specs += [
+            pl.BlockSpec((own_hidden, slots), lambda i: (0, 0)),
+            pl.BlockSpec((high, slots), lambda i: (0, 0)),
+            pl.BlockSpec((own_hidden, slots), lambda i: (1, 0)),
         ]
-        + [whole] * len(weights),
-        out_specs=pl.BlockSpec((high, tile), lambda i: (0, i)),
-        out_shape=jax.ShapeDtypeStruct((high, slots), jnp.bfloat16),
+        operands += [*earlier, hidden_grad]
+        out_shape.insert(0, jax.ShapeDtypeStruct((own_hidden, 4 * slots), jnp.bfloat16))
+    out_specs = [pl.BlockSpec(o.shape, lambda i: (0, 0)) for o in out_shape]
+    return pl.pallas_call(
+        lambda *refs: gates_kernel(len(weights), *refs),
+        grid=(1,),
+        in_specs=in_specs,
+        out_specs=out_specs,
+        out_shape=out_shape,
         cost_estimate=pl.CostEstimate(
             flops=2 * high * width * slots,
             bytes_accessed=2 * (high * width + slots * width + 2 * high * slots),
-            transcendentals=high // 2 * slots,
+            transcendentals=own_hidden * slots,
         ),
         compiler_params=pltpu.CompilerParams(vmem_limit_bytes=56 * MIB),
-    )(rows, hidden_grad, *weights)
+    )(*operands)
 
 
 def part_kernel(own_ref, *refs):
     weights, out_ref = refs[:-1], refs[-1]
+    groups, _, low, _ = out_ref.shape
     depth = weights[0].shape[1]
     own = own_ref[...].T
     for d, weight in enumerate(weights):
-        out_ref[:, d * depth : (d + 1) * depth] = jnp.dot(
-            own, weight[...], preferred_element_type=jnp.float32
-        ).astype(out_ref.dtype)
-
-
-def slot_parts(own, weights, tile):
+        out_ref[:, 0, :, d * depth : (d + 1) * depth] = (
+            jnp.dot(own, weight[...], preferred_element_type=jnp.float32)
+            .astype(out_ref.dtype)
+            .reshape(groups, low, depth)
+        )
+
+
+def slot_parts(own, weights, groups, low):
     high, slots = own.shape
+    lots = slots // (groups * low)
     width = weights[0].shape[1] * len(weights)
     whole = pl.BlockSpec(weights[0].shape, lambda i: (0, 0))
     return pl.pallas_call(
         part_kernel,
-        grid=(slots // tile,),
-        in_specs=[pl.BlockSpec((high, tile), lambda i: (0, i))] + [whole] * len(weights),
-        out_specs=pl.BlockSpec((tile, width), lambda i: (i, 0)),
-        out_shape=jax.ShapeDtypeStruct((slots, width), jnp.bfloat16),
+        grid=(lots,),
+        in_specs=[pl.BlockSpec((high, groups * low), lambda i: (0, i))] + [whole] * len(weights),
+        out_specs=pl.BlockSpec((groups, 1, low, width), lambda i: (0, i, 0, 0)),
+        out_shape=jax.ShapeDtypeStruct((groups, lots, low, width), jnp.bfloat16),
         cost_estimate=pl.CostEstimate(
             flops=2 * high * width * slots,
             bytes_accessed=2 * (high * width + slots * width + high * slots),
@@ -370,21 +395,15 @@
 
     tiles = arrived.reshape(groups, capacity // low, low, width)
     tile = lot_slots[0]
-    own, parts, back = {}, {}, {}
-    for lot in (0, 1):
-        own[lot] = hidden_gates(weights, tiles, *lots[lot], grads_first, lot, tile)
-        parts[lot] = slot_parts(own[lot], weights, tile)
-    back[0] = give_back(parts[0])
-    grads_second, parts[1], back[0] = lax.optimization_barrier((grads_second, parts[1], back[0]))
-    back[1] = give_back(parts[1])
-    own[2] = hidden_gates(weights, tiles, *lots[2], grads_second[:own_hidden], 0, tile)
-    parts[2] = slot_parts(own[2], weights, tile)
-    parts[2], back[1] = lax.optimization_barrier((parts[2], back[1]))
-    back[2] = give_back(parts[2])
-
-    shown = jnp.concatenate(
-        [own[lot][:own_hidden] for lot in range(3)] + [grads_second[own_hidden:]], axis=1
-    )
+    (first,) = hidden_gates(weights, tiles, 0, grads_first, 0)
+    back_first = give_back(slot_parts(first, weights, groups, low))
+    (second,) = hidden_gates(weights, tiles, 1, grads_first, 1)
+    grads_second, second, back_first = lax.optimization_barrier(
+        (grads_second, second, back_first)
+    )
+    shown, later = hidden_gates(weights, tiles, 2, grads_second, 0, (first, second))
+    back_later = give_back(slot_parts(later, weights, groups, low))
+
     shown = lax.all_gather(shown, "replica", axis=0, tiled=True)
     slots = sum(lot_slots)
     placed = (here - block_ids[0] // local_blocks) % shares
@@ -417,8 +436,10 @@
     )
 
     placing = placing.reshape(experts, capacity, tok_rows)
+    placing_first = placing[:, :low].reshape(-1, tok_rows).T
+    placing_later = placing[:, low:].reshape(-1, tok_rows).T
     combined = combine(
-        [(lot_of(placing, lot).T, back[lot]) for lot in range(3)], behind, sides
+        [(placing_first, back_first), (placing_later, back_later)], behind, sides
     )
     combined = combined.reshape(sides * shares, tok_rows // sides, features)
     collected = lax.all_to_all(

time: 312 us -> 312 us (level)
  waiting for transfers between devices: 146 us -> 157 us
  starting transfers between devices: 59.2 us -> 53.4 us
  Pallas kernels: 52.1 us -> 48.5 us
    all_to_all x3 -> x2, waiting for transfers between devices: 39.3 us -> 48.6 us  [give_back(): lax.all_to_all(parts, 'expert', split_axis=0, concat_axis=0, tiled=True)]
    all_to_all x3 -> x2, starting transfers between devices: 16.6 us -> 11 us  [give_back(): lax.all_to_all(parts, 'expert', split_axis=0, concat_axis=0, tiled=True)]
    pallas_call x6 -> x5, Pallas kernels: 31 us -> 28.2 us  [the longest x3 15.8 us: hidden_gates(): pl.pallas_call(lambda *refs: gates_kernel(len(weights), *refs), grid=(1,)...]
  transfers between devices with their start and end apart: 17 -> 16, of which waited for: 13 -> 12; matrix products, arithmetic and copies ran while one was open for 8% -> 9% of each run, Pallas kernels for 15% -> 14%
where the time goes in v3:
time: 312 us; the launch traced here: 311 us
  waiting for transfers between devices  157 us (50%)
  starting transfers between devices  53.4 us (17%)
  Pallas kernels  48.5 us (16%)
  between operations  18.1 us (6%)
  local copies, waits for them, and re-layouts  15.5 us (5%)
  matrix products  11.7 us (4%)
  other arithmetic  7.04 us (2%)
    ppermute x7, waiting for transfers between devices, hand_out(): return lax.ppermute(pieces[d], 'replica', shift_by(d, shares))  85.6 us
    all_to_all x2, waiting for transfers between devices, give_back(): lax.all_to_all(parts, 'expert', split_axis=0, concat_axis=0, tiled=True)  48.6 us
    ppermute x7, starting transfers between devices, hand_out(): return lax.ppermute(pieces[d], 'replica', shift_by(d, shares))  23.4 us
    pallas_call x3, Pallas kernels, hidden_gates(): pl.pallas_call(lambda *refs: gates_kernel(len(weights), *refs), grid=(1,)...  15.8 us
    pallas_call x2, Pallas kernels, slot_parts(): pl.pallas_call(part_kernel, grid=(lots,), in_specs=[pl.BlockSpec((high, g...  12.4 us
    all_to_all x1, waiting for transfers between devices, body(): lax.all_to_all(combined, ('tensor', 'replica'), split_axis=0, concat_axis...  12.2 us
    all_to_all x2, starting transfers between devices, give_back(): lax.all_to_all(parts, 'expert', split_axis=0, concat_axis=0, tiled=True)  11 us
    pallas_call x2, Pallas kernels, hidden_product(): pl.pallas_call(hidden_kernel, grid=(steps,), in_specs=[pl.BlockSpec((high...  9.22 us
  transfers between devices with their start and end apart: 16, of which 12 were waited for; matrix products, arithmetic and copies ran while one was open for 9% of the time, Pallas kernels for 14%

profile of v3, /device:TPU:8, one launch (start us, length us, event | category | flops | bytes accessed | tf_op | source)
XLA Modules:
  0.0 310.9 jit_solution(14092414473800755433)
XLA Ops:
  7.2 1.6 pad.8
  8.9 6.8 %shard_map.112 = (bf16[672,384]{1,0:T(8,128)(2,1)}, bf16[672,384]{1,0:T(8,128)(2,1)}, bf16[672,384]{1,0:T(8,128)(2,1)}, bf16[672,384]{1,0:T(8,128)(2,1)}, bf16[6...) custom-call(s32[1]{0:T(128)} %bitcast.refs_0_, ...), custom_call_target="tpu_custom_call" | custom-call | bytes 8257536 | tf_op jit(solution)/shard_map/pallas_call | solution.py:53
  16.0 1.2 reduce-window.6
  18.8 1.1 select_reduce_fusion
  19.9 1.1 fusion.6
  21.0 6.2 %all-to-all-start = ((bf16[16,48,384]{2,1,0:T(8,128)(2,1)}), bf16[16,48,384]{2,1,0:T(8,128)(2,1)}, u32[]{:S(2)}, u32[]{:S(2)}) async-start(bf16[16,48,384]{2,1,0:T(8,128)(2,1)} %bitcast.94), calls=%async_computation | async-start | bytes 1179648 | tf_op jit(solution)/shard_map/all_to_all | solution.py:369
  27.2 6.9 %collective-permute-start.4 = (bf16[672,384]{1,0:T(8,128)(2,1)}, bf16[672,384]{1,0:T(8,128)(2,1)}, u32[]{:S(2)}, u32[]{:S(2)}) collective-permute-start(bf16[672,384]{1,0:T(8,128)(2,1)} %get-tuple-element.67), channel_id=1, source_target_pairs={{0,4},{1,5},{2,6},{3,7},{4,0},{5,1},{6,2},{7,3},{8,12},{9,13},{10,... | collective-permute-start | bytes 1548296 | tf_op jit(solution)/shard_map/ppermute | solution.py:347
  34.1 3.2 %all-to-all-done = bf16[16,48,384]{2,1,0:T(8,128)(2,1)} async-done(((bf16[16,48,384]{2,1,0:T(8,128)(2,1)}), bf16[16,48,384]{2,1,0:T(8,128)(2,1)}, u32[]{:S(2)}, u32[]{:S(2)}) %all-to-all-start) | async-done | bytes 589856 | tf_op jit(solution)/shard_map/all_to_all | solution.py:369
  37.4 1.9 fusion.22
  39.3 4.8 %shard_map.115 = bf16[2688,512]{1,0:T(8,128)(2,1)} custom-call(bf16[2688,384]{1,0:T(8,128)(2,1)S(1)} %bitcast.81, bf16[512,384]{1,0:T(8,128)(2,1)S(1)} %pad_maximum_fusion.1.rows_ref), custom_call_target="tpu_custom_call" | custom-call | flops 1056964608 | bytes 7962624 | tf_op jit(solution)/shard_map/pallas_call | solution.py:156
  44.1 14.6 %collective-permute-done.4.refs_6_.refs_4_ = bf16[672,384]{1,0:T(8,128)(2,1)} collective-permute-done((bf16[672,384]{1,0:T(8,128)(2,1)}, bf16[672,384]{1,0:T(8,128)(2,1)}, u32[]{:S(2)}, u32[]{:S(2)}) %collective-permute-start.4) | collective-permute-done | bytes 516128 | tf_op jit(solution)/shard_map/ppermute | solution.py:347
  58.7 6.9 %collective-permute-start = (bf16[672,384]{1,0:T(8,128)(2,1)}, bf16[672,384]{1,0:T(8,128)(2,1)}, u32[]{:S(2)}, u32[]{:S(2)}) collective-permute-start(bf16[672,384]{1,0:T(8,128)(2,1)} %get-tuple-element.59), channel_id=1, source_target_pairs={{0,1},{1,2},{2,3},{3,4},{4,5},{5,6},{6,7},{7,0},{8,9},{9,10},{10,1... | collective-permute-start | bytes 1548296 | tf_op jit(solution)/shard_map/ppermute | solution.py:347
  66.0 0.9 copy-done.9
  67.0 4.4 %shard_map.114 = bf16[5376,256]{1,0:T(8,128)(2,1)} custom-call(bf16[2688,384]{1,0:T(8,128)(2,1)S(1)} %bitcast.82, bf16[256,384]{1,0:T(8,128)(2,1)S(1)} %bitcast.86, bf16[2688,256]{1,0:T(8,128)(2,1)S(1)} %shard_map.113.refs_0_), custom_call_target="tpu_custom_call" | custom-call | flops 528482304 | bytes 7766016 | tf_op jit(solution)/shard_map/pallas_call | solution.py:156
  71.4 1.2 slice.64
  73.9 3.5 %convolution_convert_fusion = bf16[768,3072]{1,0:T(8,128)(2,1)} fusion(pred[768,128]{1,0:T(8,128)(4,1)S(1)} %copy-done.15, bf16[128,3072]{0,1:T(8,128)(2,1)S(1)} %bitcast.92), kind=kOutput, calls=%fused_computation.1 | convolution fusion | flops 606339072 | bytes 5603328 | tf_op jit(solution)/shard_map/dot_general | solution.py:380
  77.7 1.4 collective-permute-done.1.refs_9_.refs_7_
  79.0 5.8 %all-to-all-start.1 = ((bf16[16,48,3072]{2,1,0:T(8,128)(2,1)}), bf16[16,48,3072]{2,1,0:T(8,128)(2,1)}, u32[]{:S(2)}, u32[]{:S(2)}) async-start(bf16[16,48,3072]{2,1,0:T(8,128)(2,1)} %bitcast.89), calls=%async_computation.1 | async-start | bytes 9437184 | tf_op jit(solution)/shard_map/all_to_all | solution.py:385
  84.9 1.2 collective-permute-start.2
  86.1 4.2 %collective-permute-start.3 = (bf16[672,384]{1,0:T(8,128)(2,1)}, bf16[672,384]{1,0:T(8,128)(2,1)S(1)}, u32[]{:S(2)}, u32[]{:S(2)}) collective-permute-start(bf16[672,384]{1,0:T(8,128)(2,1)} %get-tuple-element.66), channel_id=1, source_target_pairs={{0,3},{1,4},{2,5},{3,6},{4,7},{5,0},{6,1},{7,2},{8,11},{9,12},{10,... | collective-permute-start | bytes 1548296 | tf_op jit(solution)/shard_map/ppermute | solution.py:347
  90.3 0.8 collective-permute-start.5
  91.1 3.0 collective-permute-start.6
  94.2 29.8 %collective-permute-done.2.refs_4_.refs_2_ = bf16[672,384]{1,0:T(8,128)(2,1)S(1)} collective-permute-done((bf16[672,384]{1,0:T(8,128)(2,1)}, bf16[672,384]{1,0:T(8,128)(2,1)S(1)}, u32[]{:S(2)}, u32[]{:S(2)}) %collective-permute-start.2) | collective-permute-done | bytes 516128 | tf_op jit(solution)/shard_map/ppermute | solution.py:347
  124.0 38.8 %collective-permute-done.3.refs_5_.refs_3_ = bf16[672,384]{1,0:T(8,128)(2,1)S(1)} collective-permute-done((bf16[672,384]{1,0:T(8,128)(2,1)}, bf16[672,384]{1,0:T(8,128)(2,1)S(1)}, u32[]{:S(2)}, u32[]{:S(2)}) %collective-permute-start.3) | collective-permute-done | bytes 516128 | tf_op jit(solution)/shard_map/ppermute | solution.py:347
  162.8 0.8 collective-permute-done.6.refs_8_.refs_6_
  164.3 5.0 %shard_map.117.own_ref.refs_10_ = bf16[672,256]{1,0:T(8,128)(2,1)} custom-call(bf16[16,3,16,3072]{3,2,1,0:T(8,128)(2,1)} %bitcast.19.refs_0_, bf16[336,512]{1,0:T(8,128)(2,1)} %reduce-scatter.5.cloned.1.call-done.refs_1_, bf16[672,384]{1,0:T(8,128)(2,1)} %get-tuple-element.75.refs_2_.refs_0_, bf16[672,384]{1,0:T(8,128)(2,1)} %collective-permute-done.refs_3_.refs_1_, ...), custom_call_target="tpu_custom_call" | custom-call | flops 1056964608 | bytes 6389760 | tf_op jit(solution)/shard_map/pallas_call | solution.py:228
  169.4 5.2 %shard_map.118 = bf16[16,1,16,3072]{3,2,1,0:T(8,128)(2,1)} custom-call(bf16[672,256]{1,0:T(8,128)(2,1)} %shard_map.117.own_ref.refs_10_, bf16[672,384]{1,0:T(8,128)(2,1)} %get-tuple-element.75.refs_2_.refs_0_, bf16[672,384]{1,0:T(8,128)(2,1)} %collective-permute-done.refs_3_.refs_1_, bf16[672,384]{1,0:T(8,128)(2,1)} %copy-done.10, ...), custom_call_target="tpu_custom_call" | custom-call | flops 1056964608 | bytes 6045696 | tf_op jit(solution)/shard_map/pallas_call | solution.py:261
  174.6 5.3 %all-to-all-start.2 = ((bf16[16,16,3072]{2,1,0:T(8,128)(2,1)}), bf16[16,16,3072]{2,1,0:T(8,128)(2,1)S(1)}, u32[]{:S(2)}, u32[]{:S(2)}) async-start(bf16[16,16,3072]{2,1,0:T(8,128)(2,1)} %bitcast.91), calls=%async_computation.4 | async-start | bytes 3145728 | tf_op jit(solution)/shard_map/all_to_all | solution.py:393
  179.9 5.1 %shard_map.116.refs_11_ = bf16[672,256]{1,0:T(8,128)(2,1)} custom-call(bf16[16,3,16,3072]{3,2,1,0:T(8,128)(2,1)} %bitcast.19.refs_0_, bf16[336,512]{1,0:T(8,128)(2,1)} %reduce-scatter.5.cloned.1.call-done.refs_1_, bf16[672,384]{1,0:T(8,128)(2,1)} %get-tuple-element.75.refs_2_.refs_0_, bf16[672,384]{1,0:T(8,128)(2,1)} %collective-permute-done.refs_3_.refs_1_, ...), custom_call_target="tpu_custom_call" | custom-call | flops 1056964608 | bytes 6389760 | tf_op jit(solution)/shard_map/pallas_call | solution.py:228
  185.1 16.1 %all-to-all-done.2 = bf16[16,16,3072]{2,1,0:T(8,128)(2,1)S(1)} async-done(((bf16[16,16,3072]{2,1,0:T(8,128)(2,1)}), bf16[16,16,3072]{2,1,0:T(8,128)(2,1)S(1)}, u32[]{:S(2)}, u32[]{:S(2)}) %all-to-all-start.2) | async-done | bytes 1572896 | tf_op jit(solution)/shard_map/all_to_all | solution.py:393
  201.1 6.8 %reduce-scatter.3.cloned.1.call-done.refs_1_.refs_12_ = bf16[672,256]{1,0:T(8,128)(2,1)} async-done(((bf16[5376,256]{1,0:T(8,128)(2,1)}), bf16[672,256]{1,0:T(8,128)(2,1)}) %reduce-scatter.3.cloned.1.call-update) | async-done | bytes 344080 | tf_op jit(solution)/shard_map/reduce_scatter | solution.py:389
  207.9 5.6 %shard_map.119 = (bf16[336,1024]{1,0:T(8,128)(2,1)}, bf16[672,512]{1,0:T(8,128)(2,1)}) custom-call(bf16[16,3,16,3072]{3,2,1,0:T(8,128)(2,1)} %bitcast.19.refs_0_, bf16[672,256]{1,0:T(8,128)(2,1)} %reduce-scatter.3.cloned.1.call-done.refs_1_.refs_12_, bf16[672,384]{1,0:T(8,128)(2,1)} %get-tuple-element.75.refs_2_.refs_0_, ...), custom_call_target="tpu_custom_call" | custom-call | flops 1056964608 | bytes 6389760 | tf_op jit(solution)/shard_map/pallas_call | solution.py:228
  213.6 7.2 %shard_map.120 = bf16[16,2,16,3072]{3,2,1,0:T(8,128)(2,1)} custom-call(bf16[672,512]{1,0:T(8,128)(2,1)} %get-tuple-element.86.own_ref, bf16[672,384]{1,0:T(8,128)(2,1)} %get-tuple-element.75.refs_2_.refs_0_, bf16[672,384]{1,0:T(8,128)(2,1)} %collective-permute-done.refs_3_.refs_1_, bf16[672,384]{1,0:T(8,128)(2,1)} %copy-done.10, ...), custom_call_target="tpu_custom_call" | custom-call | flops 2113929216 | bytes 7962624 | tf_op jit(solution)/shard_map/pallas_call | solution.py:261
  220.8 5.7 %all-to-all-start.3 = ((bf16[16,32,3072]{2,1,0:T(8,128)(2,1)}), bf16[16,32,3072]{2,1,0:T(8,128)(2,1)S(1)}, u32[]{:S(2)}, u32[]{:S(2)}) async-start(bf16[16,32,3072]{2,1,0:T(8,128)(2,1)} %bitcast.90), calls=%async_computation.5 | async-start | bytes 6291456 | tf_op jit(solution)/shard_map/all_to_all | solution.py:393
  230.6 0.9 copy.44
  233.0 1.1 slice.55
  234.1 1.3 constant_dynamic-slice_fusion.1
  235.7 1.2 fusion.8
  236.8 32.5 %all-to-all-done.3 = bf16[16,32,3072]{2,1,0:T(8,128)(2,1)S(1)} async-done(((bf16[16,32,3072]{2,1,0:T(8,128)(2,1)}), bf16[16,32,3072]{2,1,0:T(8,128)(2,1)S(1)}, u32[]{:S(2)}, u32[]{:S(2)}) %all-to-all-start.3) | async-done | bytes 3145760 | tf_op jit(solution)/shard_map/all_to_all | solution.py:393
  269.3 1.4 copy-done.6
  270.7 1.6 shard_map.121
  272.3 0.9 copy-done.8
  273.2 6.8 %all-to-all-start.4 = ((bf16[16,64,384]{2,1,0:T(8,128)(2,1)}), bf16[16,64,384]{2,1,0:T(8,128)(2,1)S(1)}, u32[]{:S(2)}, u32[]{:S(2)}) async-start(bf16[16,64,384]{2,1,0:T(8,128)(2,1)} %bitcast.85), calls=%async_computation.6 | async-start | bytes 1572864 | tf_op jit(solution)/shard_map/all_to_all | solution.py:445
  280.3 7.0 %fusion.24.products_ref = f32[640,2688]{1,0:T(8,128)S(1)} fusion(bf16[1024,640]{1,0:T(8,128)(2,1)} %fusion.8, bf16[2688,1024]{1,0:T(8,128)(2,1)} %all-gather.4.cloned.1.call-done.packed_ref), kind=kOutput, calls=%fused_computation.62 | convolution fusion | flops 3523215360 | bytes 13697024 | tf_op jit(solution)/shard_map/sd,fs->df/dot_general | solution.py:422
  287.3 2.0 shard_map.122
  289.4 2.0 fusion.1
  291.4 12.2 %all-to-all-done.4 = bf16[16,64,384]{2,1,0:T(8,128)(2,1)S(1)} async-done(((bf16[16,64,384]{2,1,0:T(8,128)(2,1)}), bf16[16,64,384]{2,1,0:T(8,128)(2,1)S(1)}, u32[]{:S(2)}, u32[]{:S(2)}) %all-to-all-start.4) | async-done | bytes 786464 | tf_op jit(solution)/shard_map/all_to_all | solution.py:445
  303.6 0.7 reduce_sum.35
  (84 shorter events, 7.0 us)
Async XLA Ops:
  7.2 12.7 %copy-start = (bf16[128,384]{1,0:T(8,128)(2,1)S(1)}, bf16[128,384]{1,0:T(8,128)(2,1)}, u32[]{:S(2)}) copy-start(bf16[128,384]{1,0:T(8,128)(2,1)} %param.10) | copy-start | bytes 294916
  7.2 64.2 %all-gather.6.cloned.1.call-start = ((), (), s32[]{:S(2)}) async-start(), calls=%async_computation.10 | async-start | bytes 1216512 | tf_op jit(solution)/shard_map/all_gather | solution.py:352
  8.8 6.9 %copy-start.16 = (s32[128,4]{0,1:T(4,128)S(1)}, s32[128,4]{0,1:T(4,128)}, u32[]{:S(2)}) copy-start(s32[128,4]{0,1:T(4,128)} %param.12) | copy-start | bytes 6148
  8.8 8.9 %copy-start.17 = (s32[1,2]{1,0:T(1,128)S(1)}, s32[1,2]{1,0:T(1,128)}, u32[]{:S(2)}) copy-start(s32[1,2]{1,0:T(1,128)} %param.16) | copy-start | bytes 28
  8.8 8.9 %copy-start.3 = (bf16[1,384,2688]{2,1,0:T(8,128)(2,1)S(1)}, bf16[1,384,2688]{2,1,0:T(8,128)(2,1)}, u32[]{:S(2)}) copy-start(bf16[1,384,2688]{2,1,0:T(8,128)(2,1)} %param.17) | copy-start | bytes 6193156
  18.5 20.7 %copy-start.2 = (bf16[1,2688,384]{2,1,0:T(8,128)(2,1)S(1)}, bf16[1,2688,384]{2,1,0:T(8,128)(2,1)}, u32[]{:S(2)}) copy-start(bf16[1,2688,384]{2,1,0:T(8,128)(2,1)} %param.15) | copy-start | bytes 6193156
  18.8 1.1 copy-start.14
  21.0 16.3 %all-to-all-start = ((bf16[16,48,384]{2,1,0:T(8,128)(2,1)}), bf16[16,48,384]{2,1,0:T(8,128)(2,1)}, u32[]{:S(2)}, u32[]{:S(2)}) async-start(bf16[16,48,384]{2,1,0:T(8,128)(2,1)} %bitcast.94), calls=%async_computation | async-start | bytes 1179648 | tf_op jit(solution)/shard_map/all_to_all | solution.py:369
  27.2 136.4 %reduce-scatter.5.cloned.1.call-start = ((), (), s32[]{:S(2)}) async-start(), calls=%async_computation.8 | async-start | bytes 3096576 | tf_op jit(solution)/shard_map/reduce_scatter | solution.py:375
  27.2 31.4 %collective-permute-start.4 = (bf16[672,384]{1,0:T(8,128)(2,1)}, bf16[672,384]{1,0:T(8,128)(2,1)}, u32[]{:S(2)}, u32[]{:S(2)}) collective-permute-start(bf16[672,384]{1,0:T(8,128)(2,1)} %get-tuple-element.67), channel_id=1, source_target_pairs={{0,4},{1,5},{2,6},{3,7},{4,0},{5,1},{6,2},{7,3},{8,12},{9,13},{10,... | collective-permute-start | bytes 1548296 | tf_op jit(solution)/shard_map/ppermute | solution.py:347
  58.7 19.0 %collective-permute-start = (bf16[672,384]{1,0:T(8,128)(2,1)}, bf16[672,384]{1,0:T(8,128)(2,1)}, u32[]{:S(2)}, u32[]{:S(2)}) collective-permute-start(bf16[672,384]{1,0:T(8,128)(2,1)} %get-tuple-element.59), channel_id=1, source_target_pairs={{0,1},{1,2},{2,3},{3,4},{4,5},{5,6},{6,7},{7,0},{8,9},{9,10},{10,1... | collective-permute-start | bytes 1548296 | tf_op jit(solution)/shard_map/ppermute | solution.py:347
  65.6 13.4 %collective-permute-start.1 = (bf16[672,384]{1,0:T(8,128)(2,1)}, bf16[672,384]{1,0:T(8,128)(2,1)}, u32[]{:S(2)}, u32[]{:S(2)}) collective-permute-start(bf16[672,384]{1,0:T(8,128)(2,1)} %get-tuple-element.60), channel_id=1, source_target_pairs={{0,7},{1,0},{2,1},{3,2},{4,3},{5,4},{6,5},{7,6},{8,15},{9,8},{10,9... | collective-permute-start | bytes 1548296 | tf_op jit(solution)/shard_map/ppermute | solution.py:347
  66.0 0.9 copy-start.9
  72.6 1.3 copy-start.15
  79.0 11.3 %copy-start.19 = (bf16[672,384]{1,0:T(8,128)(2,1)S(1)}, bf16[672,384]{1,0:T(8,128)(2,1)}, u32[]{:S(2)}) copy-start(bf16[672,384]{1,0:T(8,128)(2,1)} %get-tuple-element.69) | copy-start | bytes 1548292
  79.0 12.1 %copy-start.18 = (bf16[672,384]{1,0:T(8,128)(2,1)S(1)}, bf16[672,384]{1,0:T(8,128)(2,1)}, u32[]{:S(2)}) copy-start(bf16[672,384]{1,0:T(8,128)(2,1)} %get-tuple-element.70) | copy-start | bytes 1548292
  79.0 84.5 %all-to-all-start.1 = ((bf16[16,48,3072]{2,1,0:T(8,128)(2,1)}), bf16[16,48,3072]{2,1,0:T(8,128)(2,1)}, u32[]{:S(2)}, u32[]{:S(2)}) async-start(bf16[16,48,3072]{2,1,0:T(8,128)(2,1)} %bitcast.89), calls=%async_computation.1 | async-start | bytes 9437184 | tf_op jit(solution)/shard_map/all_to_all | solution.py:385
  84.9 123.0 %reduce-scatter.3.cloned.1.call-start = ((), (), s32[]{:S(2)}) async-start(), calls=%async_computation.7 | async-start | bytes 3096576 | tf_op jit(solution)/shard_map/reduce_scatter | solution.py:389
  84.9 39.0 %collective-permute-start.2 = (bf16[672,384]{1,0:T(8,128)(2,1)}, bf16[672,384]{1,0:T(8,128)(2,1)S(1)}, u32[]{:S(2)}, u32[]{:S(2)}) collective-permute-start(bf16[672,384]{1,0:T(8,128)(2,1)} %get-tuple-element.65), channel_id=1, source_target_pairs={{0,2},{1,3},{2,4},{3,5},{4,6},{5,7},{6,0},{7,1},{8,10},{9,11},{10,... | collective-permute-start | bytes 1548296 | tf_op jit(solution)/shard_map/ppermute | solution.py:347
  86.1 76.7 %collective-permute-start.3 = (bf16[672,384]{1,0:T(8,128)(2,1)}, bf16[672,384]{1,0:T(8,128)(2,1)S(1)}, u32[]{:S(2)}, u32[]{:S(2)}) collective-permute-start(bf16[672,384]{1,0:T(8,128)(2,1)} %get-tuple-element.66), channel_id=1, source_target_pairs={{0,3},{1,4},{2,5},{3,6},{4,7},{5,0},{6,1},{7,2},{8,11},{9,12},{10,... | collective-permute-start | bytes 1548296 | tf_op jit(solution)/shard_map/ppermute | solution.py:347
  90.3 72.4 %collective-permute-start.5 = (bf16[672,384]{1,0:T(8,128)(2,1)S(1)}, bf16[672,384]{1,0:T(8,128)(2,1)S(1)}, u32[]{:S(2)}, u32[]{:S(2)}) collective-permute-start(bf16[672,384]{1,0:T(8,128)(2,1)S(1)} %copy-done.19), channel_id=1, source_target_pairs={{0,5},{1,6},{2,7},{3,0},{4,1},{5,2},{6,3},{7,4},{8,13},{9,14},{10,... | collective-permute-start | bytes 1548296 | tf_op jit(solution)/shard_map/ppermute | solution.py:347
  91.1 72.4 %collective-permute-start.6 = (bf16[672,384]{1,0:T(8,128)(2,1)S(1)}, bf16[672,384]{1,0:T(8,128)(2,1)S(1)}, u32[]{:S(2)}, u32[]{:S(2)}) collective-permute-start(bf16[672,384]{1,0:T(8,128)(2,1)S(1)} %copy-done.18), channel_id=1, source_target_pairs={{0,6},{1,7},{2,0},{3,1},{4,2},{5,3},{6,4},{7,5},{8,14},{9,15},{10,... | collective-permute-start | bytes 1548296 | tf_op jit(solution)/shard_map/ppermute | solution.py:347
  124.0 39.7 %copy-start.10 = (bf16[672,384]{1,0:T(8,128)(2,1)}, bf16[672,384]{1,0:T(8,128)(2,1)S(1)}, u32[]{:S(2)}) copy-start(bf16[672,384]{1,0:T(8,128)(2,1)S(1)} %collective-permute-done.2.refs_4_.refs_2_) | copy-start | bytes 1548292
  162.8 0.9 copy-start.11
  162.8 1.0 copy-start.12
  163.5 0.8 copy-start.13
  174.6 26.5 %all-to-all-start.2 = ((bf16[16,16,3072]{2,1,0:T(8,128)(2,1)}), bf16[16,16,3072]{2,1,0:T(8,128)(2,1)S(1)}, u32[]{:S(2)}, u32[]{:S(2)}) async-start(bf16[16,16,3072]{2,1,0:T(8,128)(2,1)} %bitcast.91), calls=%async_computation.4 | async-start | bytes 3145728 | tf_op jit(solution)/shard_map/all_to_all | solution.py:393
  179.9 100.4 %all-gather.4.cloned.1.call-start = ((), (), s32[]{:S(2)}) async-start(), calls=%async_computation.9 | async-start | bytes 6193152 | tf_op jit(solution)/shard_map/all_gather | solution.py:407
  201.1 12.5 %copy-start.5 = (bf16[16,16,3072]{2,1,0:T(8,128)(2,1)}, bf16[16,16,3072]{2,1,0:T(8,128)(2,1)S(1)}, u32[]{:S(2)}) copy-start(bf16[16,16,3072]{2,1,0:T(8,128)(2,1)S(1)} %all-to-all-done.2) | copy-start | bytes 4718596
  220.8 48.5 %all-to-all-start.3 = ((bf16[16,32,3072]{2,1,0:T(8,128)(2,1)}), bf16[16,32,3072]{2,1,0:T(8,128)(2,1)S(1)}, u32[]{:S(2)}, u32[]{:S(2)}) async-start(bf16[16,32,3072]{2,1,0:T(8,128)(2,1)} %bitcast.90), calls=%async_computation.5 | async-start | bytes 6291456 | tf_op jit(solution)/shard_map/all_to_all | solution.py:393
  269.3 1.4 copy-start.6
  272.3 0.9 copy-start.8
  273.2 30.4 %all-to-all-start.4 = ((bf16[16,64,384]{2,1,0:T(8,128)(2,1)}), bf16[16,64,384]{2,1,0:T(8,128)(2,1)S(1)}, u32[]{:S(2)}, u32[]{:S(2)}) async-start(bf16[16,64,384]{2,1,0:T(8,128)(2,1)} %bitcast.85), calls=%async_computation.6 | async-start | bytes 1572864 | tf_op jit(solution)/shard_map/all_to_all | solution.py:445
  280.3 7.0 %copy-start.7 = (bf16[2688,1024]{1,0:T(8,128)(2,1)S(1)}, bf16[2688,1024]{1,0:T(8,128)(2,1)}, u32[]{:S(2)}) copy-start(bf16[2688,1024]{1,0:T(8,128)(2,1)} %all-gather.4.cloned.1.call-done.packed_ref) | copy-start | bytes 16515076
  287.3 2.0 copy-start.4
  289.4 15.0 %copy-start.1 = (bf16[128,384]{1,0:T(8,128)(2,1)S(1)}, bf16[128,384]{1,0:T(8,128)(2,1)}, u32[]{:S(2)}) copy-start(bf16[128,384]{1,0:T(8,128)(2,1)} %param.10) | copy-start | bytes 294916
Sparse Core Ops, SparseCore 0:
  9.8 50.8 all-gather.5
  63.8 90.8 reduce-scatter.4
  163.7 44.1 reduce-scatter.2
  213.7 66.5 all-gather.3

commit v4 on v3

--- a/solution.py
+++ b/solution.py
@@ -193,15 +193,11 @@
     )
     grad_up = (hidden_grad * gate_pre * squashed).astype(jnp.bfloat16)
     own_ref = others[-1]
-    at = own_ref.shape[1] - slots
-    own_ref[:own_hidden, at:] = grad_gate
-    own_ref[own_hidden:, at:] = grad_up
+    own_ref[:own_hidden, :] = grad_gate
+    own_ref[own_hidden:, :] = grad_up
     if len(others) > 1:
         first_ref, second_ref, extra_ref, shown_ref, _ = others
-        own_ref[:, :at] = second_ref[...]
-        for lot, rows in enumerate(
-            (first_ref[...], second_ref[:own_hidden, :], grad_gate, extra_ref[...])
-        ):
+        for lot, rows in enumerate((first_ref[...], second_ref[...], grad_gate, extra_ref[...])):
             shown_ref[:, lot * slots : (lot + 1) * slots] = rows
 
 
@@ -209,8 +205,7 @@
     groups, _, low, width = rows.shape
     high, slots = weights[0].shape[0], groups * low
     own_hidden = high // 2
-    wide = 2 * slots if earlier else slots
-    out_shape = [jax.ShapeDtypeStruct((high, wide), jnp.bfloat16)]
+    out_shape = [jax.ShapeDtypeStruct((high, slots), jnp.bfloat16)]
     in_specs = [
         pl.BlockSpec((groups, 1, low, width), lambda i: (0, lot, 0, 0)),
         pl.BlockSpec((own_hidden, slots), lambda i: (0, at)),
@@ -219,7 +214,7 @@
     if earlier:
         in_specs += [
             pl.BlockSpec((own_hidden, slots), lambda i: (0, 0)),
-            pl.BlockSpec((high, slots), lambda i: (0, 0)),
+            pl.BlockSpec((own_hidden, slots), lambda i: (0, 0)),
             pl.BlockSpec((own_hidden, slots), lambda i: (1, 0)),
         ]
         operands += [*earlier, hidden_grad]
@@ -240,8 +235,8 @@
     )(*operands)
 
 
-def part_kernel(own_ref, *refs):
-    weights, out_ref = refs[:-1], refs[-1]
+def part_kernel(shares, own_ref, *refs):
+    weights, out_ref = refs[:shares], refs[-1]
     groups, _, low, _ = out_ref.shape
     depth = weights[0].shape[1]
     own = own_ref[...].T
@@ -253,24 +248,27 @@
         )
 
 
-def slot_parts(own, weights, groups, low):
+def slot_parts(own, weights, groups, lots, lot, earlier=None):
     high, slots = own.shape
-    lots = slots // (groups * low)
+    low = slots // groups
     width = weights[0].shape[1] * len(weights)
-    whole = pl.BlockSpec(weights[0].shape, lambda i: (0, 0))
-    return pl.pallas_call(
-        part_kernel,
-        grid=(lots,),
-        in_specs=[pl.BlockSpec((high, groups * low), lambda i: (0, i))] + [whole] * len(weights),
-        out_specs=pl.BlockSpec((groups, 1, low, width), lambda i: (0, i, 0, 0)),
+    more = [] if earlier is None else [earlier]
+    return pl.pallas_call(
+        lambda *refs: part_kernel(len(weights), *refs),
+        grid=(1,),
+        in_specs=[pl.BlockSpec((high, slots), lambda i: (0, 0))]
+        + [pl.BlockSpec(weights[0].shape, lambda i: (0, 0))] * len(weights)
+        + [pl.BlockSpec(memory_space=pl.ANY)] * len(more),
+        out_specs=pl.BlockSpec((groups, 1, low, width), lambda i: (0, lot, 0, 0)),
         out_shape=jax.ShapeDtypeStruct((groups, lots, low, width), jnp.bfloat16),
+        input_output_aliases={1 + len(weights): 0} if more else {},
         cost_estimate=pl.CostEstimate(
             flops=2 * high * width * slots,
             bytes_accessed=2 * (high * width + slots * width + high * slots),
             transcendentals=0,
         ),
         compiler_params=pltpu.CompilerParams(vmem_limit_bytes=56 * MIB),
-    )(own, *weights)
+    )(own, *weights, *more)
 
 
 def combine_kernel(behind_ref, *refs):
@@ -396,13 +394,14 @@
     tiles = arrived.reshape(groups, capacity // low, low, width)
     tile = lot_slots[0]
     (first,) = hidden_gates(weights, tiles, 0, grads_first, 0)
-    back_first = give_back(slot_parts(first, weights, groups, low))
+    back_first = give_back(slot_parts(first, weights, groups, 1, 0))
     (second,) = hidden_gates(weights, tiles, 1, grads_first, 1)
-    grads_second, second, back_first = lax.optimization_barrier(
-        (grads_second, second, back_first)
-    )
-    shown, later = hidden_gates(weights, tiles, 2, grads_second, 0, (first, second))
-    back_later = give_back(slot_parts(later, weights, groups, low))
+    parts = slot_parts(second, weights, groups, 2, 0)
+    grads_second, second, parts, back_first = lax.optimization_barrier(
+        (grads_second, second, parts, back_first)
+    )
+    shown, third = hidden_gates(weights, tiles, 2, grads_second, 0, (first, second))
+    back_later = give_back(slot_parts(third, weights, groups, 2, 1, parts))
 
     shown = lax.all_gather(shown, "replica", axis=0, tiled=True)
     slots = sum(lot_slots)

time: 312 us -> 310 us (level)
  waiting for transfers between devices: 157 us -> 151 us
  Pallas kernels: 48.5 us -> 51.8 us
    all_to_all x2, waiting for transfers between devices: 48.6 us -> 43.2 us  [give_back(): lax.all_to_all(parts, 'expert', split_axis=0, concat_axis=0, tiled=True)]
    pallas_call x2 -> x3, Pallas kernels: 12.4 us -> 15.8 us  [slot_parts(): pl.pallas_call(lambda *refs: part_kernel(len(weights), *refs), grid=(1,),...]
  transfers between devices with their start and end apart: 16 -> 16, of which waited for: 12 -> 11; matrix products, arithmetic and copies ran while one was open for 9% -> 9% of each run, Pallas kernels for 14% -> 15%
where the time goes in v4:
time: 310 us; the launch traced here: 309 us
  waiting for transfers between devices  151 us (49%)
  starting transfers between devices  53.7 us (17%)
  Pallas kernels  51.8 us (17%)
  between operations  18.1 us (6%)
  local copies, waits for them, and re-layouts  15.8 us (5%)
  matrix products  11.7 us (4%)
  other arithmetic  7.04 us (2%)
    ppermute x7, waiting for transfers between devices, hand_out(): return lax.ppermute(pieces[d], 'replica', shift_by(d, shares))  85.1 us
    all_to_all x2, waiting for transfers between devices, give_back(): lax.all_to_all(parts, 'expert', split_axis=0, concat_axis=0, tiled=True)  43.2 us
    ppermute x7, starting transfers between devices, hand_out(): return lax.ppermute(pieces[d], 'replica', shift_by(d, shares))  23.2 us
    pallas_call x3, Pallas kernels, slot_parts(): pl.pallas_call(lambda *refs: part_kernel(len(weights), *refs), grid=(1,),...  15.8 us
    pallas_call x3, Pallas kernels, hidden_gates(): pl.pallas_call(lambda *refs: gates_kernel(len(weights), *refs), grid=(1,)...  15.7 us
    all_to_all x2, starting transfers between devices, give_back(): lax.all_to_all(parts, 'expert', split_axis=0, concat_axis=0, tiled=True)  11.4 us
    all_to_all x1, waiting for transfers between devices, body(): lax.all_to_all(combined, ('tensor', 'replica'), split_axis=0, concat_axis...  10.4 us
    pallas_call x2, Pallas kernels, hidden_product(): pl.pallas_call(hidden_kernel, grid=(steps,), in_specs=[pl.BlockSpec((high...  9.15 us
  transfers between devices with their start and end apart: 16, of which 11 were waited for; matrix products, arithmetic and copies ran while one was open for 9% of the time, Pallas kernels for 15%

profile of v4, /device:TPU:8, one launch (start us, length us, event | category | flops | bytes accessed | tf_op | source)
XLA Modules:
  0.0 308.9 jit_solution(1342915950633713504)
XLA Ops:
  7.2 1.6 pad.8
  8.9 6.9 %shard_map.112 = (bf16[672,384]{1,0:T(8,128)(2,1)}, bf16[672,384]{1,0:T(8,128)(2,1)}, bf16[672,384]{1,0:T(8,128)(2,1)}, bf16[672,384]{1,0:T(8,128)(2,1)}, bf16[6...) custom-call(s32[1]{0:T(128)} %bitcast.refs_0_, ...), custom_call_target="tpu_custom_call" | custom-call | bytes 8257536 | tf_op jit(solution)/shard_map/pallas_call | solution.py:53
  16.1 1.2 reduce-window.6
  18.9 1.1 select_reduce_fusion
  20.0 1.1 fusion.6
  21.1 6.2 %all-to-all-start = ((bf16[16,48,384]{2,1,0:T(8,128)(2,1)}), bf16[16,48,384]{2,1,0:T(8,128)(2,1)}, u32[]{:S(2)}, u32[]{:S(2)}) async-start(bf16[16,48,384]{2,1,0:T(8,128)(2,1)} %bitcast.94), calls=%async_computation | async-start | bytes 1179648 | tf_op jit(solution)/shard_map/all_to_all | solution.py:367
  27.3 6.9 %collective-permute-start.4 = (bf16[672,384]{1,0:T(8,128)(2,1)}, bf16[672,384]{1,0:T(8,128)(2,1)}, u32[]{:S(2)}, u32[]{:S(2)}) collective-permute-start(bf16[672,384]{1,0:T(8,128)(2,1)} %get-tuple-element.68), channel_id=1, source_target_pairs={{0,4},{1,5},{2,6},{3,7},{4,0},{5,1},{6,2},{7,3},{8,12},{9,13},{10,... | collective-permute-start | bytes 1548296 | tf_op jit(solution)/shard_map/ppermute | solution.py:345
  34.2 3.2 %all-to-all-done = bf16[16,48,384]{2,1,0:T(8,128)(2,1)} async-done(((bf16[16,48,384]{2,1,0:T(8,128)(2,1)}), bf16[16,48,384]{2,1,0:T(8,128)(2,1)}, u32[]{:S(2)}, u32[]{:S(2)}) %all-to-all-start) | async-done | bytes 589856 | tf_op jit(solution)/shard_map/all_to_all | solution.py:367
  37.4 1.9 fusion.22
  39.3 4.8 %shard_map.115 = bf16[2688,512]{1,0:T(8,128)(2,1)} custom-call(bf16[2688,384]{1,0:T(8,128)(2,1)S(1)} %bitcast.81, bf16[512,384]{1,0:T(8,128)(2,1)S(1)} %pad_maximum_fusion.1.rows_ref), custom_call_target="tpu_custom_call" | custom-call | flops 1056964608 | bytes 7962624 | tf_op jit(solution)/shard_map/pallas_call | solution.py:156
  44.1 15.1 %collective-permute-done.4.refs_6_.refs_5_ = bf16[672,384]{1,0:T(8,128)(2,1)} collective-permute-done((bf16[672,384]{1,0:T(8,128)(2,1)}, bf16[672,384]{1,0:T(8,128)(2,1)}, u32[]{:S(2)}, u32[]{:S(2)}) %collective-permute-start.4) | collective-permute-done | bytes 516128 | tf_op jit(solution)/shard_map/ppermute | solution.py:345
  59.2 6.5 %collective-permute-start = (bf16[672,384]{1,0:T(8,128)(2,1)}, bf16[672,384]{1,0:T(8,128)(2,1)}, u32[]{:S(2)}, u32[]{:S(2)}) collective-permute-start(bf16[672,384]{1,0:T(8,128)(2,1)} %get-tuple-element.60), channel_id=1, source_target_pairs={{0,1},{1,2},{2,3},{3,4},{4,5},{5,6},{6,7},{7,0},{8,9},{9,10},{10,1... | collective-permute-start | bytes 1548296 | tf_op jit(solution)/shard_map/ppermute | solution.py:345
  66.3 0.9 copy-done.9
  67.2 4.3 %shard_map.114 = bf16[5376,256]{1,0:T(8,128)(2,1)} custom-call(bf16[2688,384]{1,0:T(8,128)(2,1)S(1)} %bitcast.82, bf16[256,384]{1,0:T(8,128)(2,1)S(1)} %bitcast.86, bf16[2688,256]{1,0:T(8,128)(2,1)S(1)} %shard_map.113.refs_0_), custom_call_target="tpu_custom_call" | custom-call | flops 528482304 | bytes 7766016 | tf_op jit(solution)/shard_map/pallas_call | solution.py:156
  71.6 1.2 slice.64
  74.1 3.5 %convolution_convert_fusion = bf16[768,3072]{1,0:T(8,128)(2,1)} fusion(pred[768,128]{1,0:T(8,128)(4,1)S(1)} %copy-done.15, bf16[128,3072]{0,1:T(8,128)(2,1)S(1)} %bitcast.92), kind=kOutput, calls=%fused_computation.1 | convolution fusion | flops 606339072 | bytes 5603328 | tf_op jit(solution)/shard_map/dot_general | solution.py:378
  77.9 1.3 collective-permute-done.1.refs_9_.refs_8_
  79.2 5.8 %all-to-all-start.1 = ((bf16[16,48,3072]{2,1,0:T(8,128)(2,1)}), bf16[16,48,3072]{2,1,0:T(8,128)(2,1)}, u32[]{:S(2)}, u32[]{:S(2)}) async-start(bf16[16,48,3072]{2,1,0:T(8,128)(2,1)} %bitcast.89), calls=%async_computation.1 | async-start | bytes 9437184 | tf_op jit(solution)/shard_map/all_to_all | solution.py:383
  85.1 1.1 collective-permute-start.2
  86.2 4.1 %collective-permute-start.3 = (bf16[672,384]{1,0:T(8,128)(2,1)}, bf16[672,384]{1,0:T(8,128)(2,1)S(1)}, u32[]{:S(2)}, u32[]{:S(2)}) collective-permute-start(bf16[672,384]{1,0:T(8,128)(2,1)} %get-tuple-element.67), channel_id=1, source_target_pairs={{0,3},{1,4},{2,5},{3,6},{4,7},{5,0},{6,1},{7,2},{8,11},{9,12},{10,... | collective-permute-start | bytes 1548296 | tf_op jit(solution)/shard_map/ppermute | solution.py:345
  90.3 0.9 collective-permute-start.5
  91.2 3.1 %collective-permute-start.6 = (bf16[672,384]{1,0:T(8,128)(2,1)S(1)}, bf16[672,384]{1,0:T(8,128)(2,1)S(1)}, u32[]{:S(2)}, u32[]{:S(2)}) collective-permute-start(bf16[672,384]{1,0:T(8,128)(2,1)S(1)} %copy-done.18), channel_id=1, source_target_pairs={{0,6},{1,7},{2,0},{3,1},{4,2},{5,3},{6,4},{7,5},{8,14},{9,15},{10,... | collective-permute-start | bytes 1548296 | tf_op jit(solution)/shard_map/ppermute | solution.py:345
  94.3 29.5 %collective-permute-done.2.refs_4_.refs_3_ = bf16[672,384]{1,0:T(8,128)(2,1)S(1)} collective-permute-done((bf16[672,384]{1,0:T(8,128)(2,1)}, bf16[672,384]{1,0:T(8,128)(2,1)S(1)}, u32[]{:S(2)}, u32[]{:S(2)}) %collective-permute-start.2) | collective-permute-done | bytes 516128 | tf_op jit(solution)/shard_map/ppermute | solution.py:345
  123.8 39.0 %collective-permute-done.3.refs_5_.refs_4_ = bf16[672,384]{1,0:T(8,128)(2,1)S(1)} collective-permute-done((bf16[672,384]{1,0:T(8,128)(2,1)}, bf16[672,384]{1,0:T(8,128)(2,1)S(1)}, u32[]{:S(2)}, u32[]{:S(2)}) %collective-permute-start.3) | collective-permute-done | bytes 516128 | tf_op jit(solution)/shard_map/ppermute | solution.py:345
  164.0 5.0 %shard_map.118.refs_0_.refs_10_ = bf16[672,256]{1,0:T(8,128)(2,1)} custom-call(bf16[16,3,16,3072]{3,2,1,0:T(8,128)(2,1)} %bitcast.19.refs_0_, bf16[336,512]{1,0:T(8,128)(2,1)} %reduce-scatter.5.cloned.1.call-done.refs_1_, bf16[672,384]{1,0:T(8,128)(2,1)} %get-tuple-element.76.refs_2_.refs_1_, bf16[672,384]{1,0:T(8,128)(2,1)} %collective-permute-done.refs_3_.refs_2_, ...), custom_call_target="tpu_custom_call" | custom-call | flops 1056964608 | bytes 6389760 | tf_op jit(solution)/shard_map/pallas_call | solution.py:223
  169.0 5.2 %shard_map.119 = bf16[16,1,16,3072]{3,2,1,0:T(8,128)(2,1)} custom-call(bf16[672,256]{1,0:T(8,128)(2,1)} %shard_map.118.refs_0_.refs_10_, bf16[672,384]{1,0:T(8,128)(2,1)} %get-tuple-element.76.refs_2_.refs_1_, bf16[672,384]{1,0:T(8,128)(2,1)} %collective-permute-done.refs_3_.refs_2_, bf16[672,384]{1,0:T(8,128)(2,1)} %copy-done.10, ...), custom_call_target="tpu_custom_call" | custom-call | flops 1056964608 | bytes 6045696 | tf_op jit(solution)/shard_map/pallas_call | solution.py:256
  174.2 5.7 %all-to-all-start.2 = ((bf16[16,16,3072]{2,1,0:T(8,128)(2,1)}), bf16[16,16,3072]{2,1,0:T(8,128)(2,1)S(1)}, u32[]{:S(2)}, u32[]{:S(2)}) async-start(bf16[16,16,3072]{2,1,0:T(8,128)(2,1)} %bitcast.91), calls=%async_computation.4 | async-start | bytes 3145728 | tf_op jit(solution)/shard_map/all_to_all | solution.py:391
  180.0 5.1 %shard_map.116.refs_0_.refs_11_ = bf16[672,256]{1,0:T(8,128)(2,1)} custom-call(bf16[16,3,16,3072]{3,2,1,0:T(8,128)(2,1)} %bitcast.19.refs_0_, bf16[336,512]{1,0:T(8,128)(2,1)} %reduce-scatter.5.cloned.1.call-done.refs_1_, bf16[672,384]{1,0:T(8,128)(2,1)} %get-tuple-element.76.refs_2_.refs_1_, bf16[672,384]{1,0:T(8,128)(2,1)} %collective-permute-done.refs_3_.refs_2_, ...), custom_call_target="tpu_custom_call" | custom-call | flops 1056964608 | bytes 6389760 | tf_op jit(solution)/shard_map/pallas_call | solution.py:223
  185.2 5.3 %shard_map.117.refs_9_ = bf16[16,2,16,3072]{3,2,1,0:T(8,128)(2,1)} custom-call(bf16[672,256]{1,0:T(8,128)(2,1)} %shard_map.116.refs_0_.refs_11_, bf16[672,384]{1,0:T(8,128)(2,1)} %get-tuple-element.76.refs_2_.refs_1_, bf16[672,384]{1,0:T(8,128)(2,1)} %collective-permute-done.refs_3_.refs_2_, bf16[672,384]{1,0:T(8,128)(2,1)} %copy-done.10, ...), custom_call_target="tpu_custom_call" | custom-call | flops 1056964608 | bytes 6045696 | tf_op jit(solution)/shard_map/pallas_call | solution.py:256
  190.5 10.7 %all-to-all-done.2 = bf16[16,16,3072]{2,1,0:T(8,128)(2,1)S(1)} async-done(((bf16[16,16,3072]{2,1,0:T(8,128)(2,1)}), bf16[16,16,3072]{2,1,0:T(8,128)(2,1)S(1)}, u32[]{:S(2)}, u32[]{:S(2)}) %all-to-all-start.2) | async-done | bytes 1572896 | tf_op jit(solution)/shard_map/all_to_all | solution.py:391
  201.2 6.6 %reduce-scatter.3.cloned.1.call-done.refs_1_.refs_12_ = bf16[672,256]{1,0:T(8,128)(2,1)} async-done(((bf16[5376,256]{1,0:T(8,128)(2,1)}), bf16[672,256]{1,0:T(8,128)(2,1)}) %reduce-scatter.3.cloned.1.call-update) | async-done | bytes 344080 | tf_op jit(solution)/shard_map/reduce_scatter | solution.py:387
  207.8 5.5 %shard_map.120 = (bf16[336,1024]{1,0:T(8,128)(2,1)}, bf16[672,256]{1,0:T(8,128)(2,1)}) custom-call(bf16[16,3,16,3072]{3,2,1,0:T(8,128)(2,1)} %bitcast.19.refs_0_, bf16[672,256]{1,0:T(8,128)(2,1)} %reduce-scatter.3.cloned.1.call-done.refs_1_.refs_12_, bf16[672,384]{1,0:T(8,128)(2,1)} %get-tuple-element.76.refs_2_.refs_1_, ...), custom_call_target="tpu_custom_call" | custom-call | flops 1056964608 | bytes 6389760 | tf_op jit(solution)/shard_map/pallas_call | solution.py:223
  213.3 5.3 %shard_map.121 = bf16[16,2,16,3072]{3,2,1,0:T(8,128)(2,1)} custom-call(bf16[672,256]{1,0:T(8,128)(2,1)} %get-tuple-element.87.refs_0_, bf16[672,384]{1,0:T(8,128)(2,1)} %get-tuple-element.76.refs_2_.refs_1_, bf16[672,384]{1,0:T(8,128)(2,1)} %collective-permute-done.refs_3_.refs_2_, bf16[672,384]{1,0:T(8,128)(2,1)} %copy-done.10, ...), custom_call_target="tpu_custom_call", output_to_operand_aliasing={{}: (9, {})} | custom-call | flops 1056964608 | bytes 6045696 | tf_op jit(solution)/shard_map/pallas_call | solution.py:256
  218.6 5.7 %all-to-all-start.3 = ((bf16[16,32,3072]{2,1,0:T(8,128)(2,1)}), bf16[16,32,3072]{2,1,0:T(8,128)(2,1)S(1)}, u32[]{:S(2)}, u32[]{:S(2)}) async-start(bf16[16,32,3072]{2,1,0:T(8,128)(2,1)} %bitcast.90), calls=%async_computation.5 | async-start | bytes 6291456 | tf_op jit(solution)/shard_map/all_to_all | solution.py:391
  228.4 0.9 copy.45
  230.8 1.1 slice.55
  232.0 1.3 constant_dynamic-slice_fusion.1
  233.5 1.2 fusion.8
  234.6 32.5 %all-to-all-done.3 = bf16[16,32,3072]{2,1,0:T(8,128)(2,1)S(1)} async-done(((bf16[16,32,3072]{2,1,0:T(8,128)(2,1)}), bf16[16,32,3072]{2,1,0:T(8,128)(2,1)S(1)}, u32[]{:S(2)}, u32[]{:S(2)}) %all-to-all-start.3) | async-done | bytes 3145760 | tf_op jit(solution)/shard_map/all_to_all | solution.py:391
  267.1 1.4 copy-done.6
  268.6 1.6 shard_map.122
  270.1 0.9 copy-done.8
  271.0 7.0 %all-to-all-start.4 = ((bf16[16,64,384]{2,1,0:T(8,128)(2,1)}), bf16[16,64,384]{2,1,0:T(8,128)(2,1)S(1)}, u32[]{:S(2)}, u32[]{:S(2)}) async-start(bf16[16,64,384]{2,1,0:T(8,128)(2,1)} %bitcast.85), calls=%async_computation.6 | async-start | bytes 1572864 | tf_op jit(solution)/shard_map/all_to_all | solution.py:444
  278.0 2.1 all-gather.4.cloned.1.call-done.packed_ref
  280.1 7.0 %fusion.24.products_ref = f32[640,2688]{1,0:T(8,128)S(1)} fusion(bf16[1024,640]{1,0:T(8,128)(2,1)} %fusion.8, bf16[2688,1024]{1,0:T(8,128)(2,1)} %all-gather.4.cloned.1.call-done.packed_ref), kind=kOutput, calls=%fused_computation.62 | convolution fusion | flops 3523215360 | bytes 13697024 | tf_op jit(solution)/shard_map/sd,fs->df/dot_general | solution.py:421
  287.2 2.0 shard_map.123
  289.2 2.0 fusion.1
  291.2 10.4 %all-to-all-done.4 = bf16[16,64,384]{2,1,0:T(8,128)(2,1)S(1)} async-done(((bf16[16,64,384]{2,1,0:T(8,128)(2,1)}), bf16[16,64,384]{2,1,0:T(8,128)(2,1)S(1)}, u32[]{:S(2)}, u32[]{:S(2)}) %all-to-all-start.4) | async-done | bytes 786464 | tf_op jit(solution)/shard_map/all_to_all | solution.py:444
  (85 shorter events, 8.0 us)
Async XLA Ops:
  7.2 12.8 %copy-start = (bf16[128,384]{1,0:T(8,128)(2,1)S(1)}, bf16[128,384]{1,0:T(8,128)(2,1)}, u32[]{:S(2)}) copy-start(bf16[128,384]{1,0:T(8,128)(2,1)} %param.10) | copy-start | bytes 294916
  7.2 64.4 %all-gather.6.cloned.1.call-start = ((), (), s32[]{:S(2)}) async-start(), calls=%async_computation.10 | async-start | bytes 1216512 | tf_op jit(solution)/shard_map/all_gather | solution.py:350
  8.8 7.0 %copy-start.16 = (s32[128,4]{0,1:T(4,128)S(1)}, s32[128,4]{0,1:T(4,128)}, u32[]{:S(2)}) copy-start(s32[128,4]{0,1:T(4,128)} %param.12) | copy-start | bytes 6148
  8.8 9.0 %copy-start.17 = (s32[1,2]{1,0:T(1,128)S(1)}, s32[1,2]{1,0:T(1,128)}, u32[]{:S(2)}) copy-start(s32[1,2]{1,0:T(1,128)} %param.16) | copy-start | bytes 28
  8.8 9.0 %copy-start.3 = (bf16[1,384,2688]{2,1,0:T(8,128)(2,1)S(1)}, bf16[1,384,2688]{2,1,0:T(8,128)(2,1)}, u32[]{:S(2)}) copy-start(bf16[1,384,2688]{2,1,0:T(8,128)(2,1)} %param.17) | copy-start | bytes 6193156
  18.6 20.7 %copy-start.2 = (bf16[1,2688,384]{2,1,0:T(8,128)(2,1)S(1)}, bf16[1,2688,384]{2,1,0:T(8,128)(2,1)}, u32[]{:S(2)}) copy-start(bf16[1,2688,384]{2,1,0:T(8,128)(2,1)} %param.15) | copy-start | bytes 6193156
  18.8 1.1 copy-start.14
  21.1 16.3 %all-to-all-start = ((bf16[16,48,384]{2,1,0:T(8,128)(2,1)}), bf16[16,48,384]{2,1,0:T(8,128)(2,1)}, u32[]{:S(2)}, u32[]{:S(2)}) async-start(bf16[16,48,384]{2,1,0:T(8,128)(2,1)} %bitcast.94), calls=%async_computation | async-start | bytes 1179648 | tf_op jit(solution)/shard_map/all_to_all | solution.py:367
  27.3 135.7 %reduce-scatter.5.cloned.1.call-start = ((), (), s32[]{:S(2)}) async-start(), calls=%async_computation.8 | async-start | bytes 3096576 | tf_op jit(solution)/shard_map/reduce_scatter | solution.py:373
  27.3 31.9 %collective-permute-start.4 = (bf16[672,384]{1,0:T(8,128)(2,1)}, bf16[672,384]{1,0:T(8,128)(2,1)}, u32[]{:S(2)}, u32[]{:S(2)}) collective-permute-start(bf16[672,384]{1,0:T(8,128)(2,1)} %get-tuple-element.68), channel_id=1, source_target_pairs={{0,4},{1,5},{2,6},{3,7},{4,0},{5,1},{6,2},{7,3},{8,12},{9,13},{10,... | collective-permute-start | bytes 1548296 | tf_op jit(solution)/shard_map/ppermute | solution.py:345
  59.2 18.7 %collective-permute-start = (bf16[672,384]{1,0:T(8,128)(2,1)}, bf16[672,384]{1,0:T(8,128)(2,1)}, u32[]{:S(2)}, u32[]{:S(2)}) collective-permute-start(bf16[672,384]{1,0:T(8,128)(2,1)} %get-tuple-element.60), channel_id=1, source_target_pairs={{0,1},{1,2},{2,3},{3,4},{4,5},{5,6},{6,7},{7,0},{8,9},{9,10},{10,1... | collective-permute-start | bytes 1548296 | tf_op jit(solution)/shard_map/ppermute | solution.py:345
  65.7 13.5 %collective-permute-start.1 = (bf16[672,384]{1,0:T(8,128)(2,1)}, bf16[672,384]{1,0:T(8,128)(2,1)}, u32[]{:S(2)}, u32[]{:S(2)}) collective-permute-start(bf16[672,384]{1,0:T(8,128)(2,1)} %get-tuple-element.61), channel_id=1, source_target_pairs={{0,7},{1,0},{2,1},{3,2},{4,3},{5,4},{6,5},{7,6},{8,15},{9,8},{10,9... | collective-permute-start | bytes 1548296 | tf_op jit(solution)/shard_map/ppermute | solution.py:345
  66.3 0.9 copy-start.9
  72.8 1.3 copy-start.15
  79.2 11.1 %copy-start.19 = (bf16[672,384]{1,0:T(8,128)(2,1)S(1)}, bf16[672,384]{1,0:T(8,128)(2,1)}, u32[]{:S(2)}) copy-start(bf16[672,384]{1,0:T(8,128)(2,1)} %get-tuple-element.70) | copy-start | bytes 1548292
  79.2 12.0 %copy-start.18 = (bf16[672,384]{1,0:T(8,128)(2,1)S(1)}, bf16[672,384]{1,0:T(8,128)(2,1)}, u32[]{:S(2)}) copy-start(bf16[672,384]{1,0:T(8,128)(2,1)} %get-tuple-element.71) | copy-start | bytes 1548292
  79.2 83.7 %all-to-all-start.1 = ((bf16[16,48,3072]{2,1,0:T(8,128)(2,1)}), bf16[16,48,3072]{2,1,0:T(8,128)(2,1)}, u32[]{:S(2)}, u32[]{:S(2)}) async-start(bf16[16,48,3072]{2,1,0:T(8,128)(2,1)} %bitcast.89), calls=%async_computation.1 | async-start | bytes 9437184 | tf_op jit(solution)/shard_map/all_to_all | solution.py:383
  85.0 122.8 %reduce-scatter.3.cloned.1.call-start = ((), (), s32[]{:S(2)}) async-start(), calls=%async_computation.7 | async-start | bytes 3096576 | tf_op jit(solution)/shard_map/reduce_scatter | solution.py:387
  85.1 38.7 %collective-permute-start.2 = (bf16[672,384]{1,0:T(8,128)(2,1)}, bf16[672,384]{1,0:T(8,128)(2,1)S(1)}, u32[]{:S(2)}, u32[]{:S(2)}) collective-permute-start(bf16[672,384]{1,0:T(8,128)(2,1)} %get-tuple-element.66), channel_id=1, source_target_pairs={{0,2},{1,3},{2,4},{3,5},{4,6},{5,7},{6,0},{7,1},{8,10},{9,11},{10,... | collective-permute-start | bytes 1548296 | tf_op jit(solution)/shard_map/ppermute | solution.py:345
  86.2 76.7 %collective-permute-start.3 = (bf16[672,384]{1,0:T(8,128)(2,1)}, bf16[672,384]{1,0:T(8,128)(2,1)S(1)}, u32[]{:S(2)}, u32[]{:S(2)}) collective-permute-start(bf16[672,384]{1,0:T(8,128)(2,1)} %get-tuple-element.67), channel_id=1, source_target_pairs={{0,3},{1,4},{2,5},{3,6},{4,7},{5,0},{6,1},{7,2},{8,11},{9,12},{10,... | collective-permute-start | bytes 1548296 | tf_op jit(solution)/shard_map/ppermute | solution.py:345
  90.3 72.6 %collective-permute-start.5 = (bf16[672,384]{1,0:T(8,128)(2,1)S(1)}, bf16[672,384]{1,0:T(8,128)(2,1)S(1)}, u32[]{:S(2)}, u32[]{:S(2)}) collective-permute-start(bf16[672,384]{1,0:T(8,128)(2,1)S(1)} %copy-done.19), channel_id=1, source_target_pairs={{0,5},{1,6},{2,7},{3,0},{4,1},{5,2},{6,3},{7,4},{8,13},{9,14},{10,... | collective-permute-start | bytes 1548296 | tf_op jit(solution)/shard_map/ppermute | solution.py:345
  91.2 71.6 %collective-permute-start.6 = (bf16[672,384]{1,0:T(8,128)(2,1)S(1)}, bf16[672,384]{1,0:T(8,128)(2,1)S(1)}, u32[]{:S(2)}, u32[]{:S(2)}) collective-permute-start(bf16[672,384]{1,0:T(8,128)(2,1)S(1)} %copy-done.18), channel_id=1, source_target_pairs={{0,6},{1,7},{2,0},{3,1},{4,2},{5,3},{6,4},{7,5},{8,14},{9,15},{10,... | collective-permute-start | bytes 1548296 | tf_op jit(solution)/shard_map/ppermute | solution.py:345
  123.8 39.1 %copy-start.10 = (bf16[672,384]{1,0:T(8,128)(2,1)}, bf16[672,384]{1,0:T(8,128)(2,1)S(1)}, u32[]{:S(2)}) copy-start(bf16[672,384]{1,0:T(8,128)(2,1)S(1)} %collective-permute-done.2.refs_4_.refs_3_) | copy-start | bytes 1548292
  162.8 0.8 copy-start.11
  162.8 1.0 copy-start.12
  162.9 1.1 copy-start.13
  174.2 27.0 %all-to-all-start.2 = ((bf16[16,16,3072]{2,1,0:T(8,128)(2,1)}), bf16[16,16,3072]{2,1,0:T(8,128)(2,1)S(1)}, u32[]{:S(2)}, u32[]{:S(2)}) async-start(bf16[16,16,3072]{2,1,0:T(8,128)(2,1)} %bitcast.91), calls=%async_computation.4 | async-start | bytes 3145728 | tf_op jit(solution)/shard_map/all_to_all | solution.py:391
  180.0 100.1 %all-gather.4.cloned.1.call-start = ((), (), s32[]{:S(2)}) async-start(), calls=%async_computation.9 | async-start | bytes 6193152 | tf_op jit(solution)/shard_map/all_gather | solution.py:406
  201.2 12.0 %copy-start.5 = (bf16[16,16,3072]{2,1,0:T(8,128)(2,1)}, bf16[16,16,3072]{2,1,0:T(8,128)(2,1)S(1)}, u32[]{:S(2)}) copy-start(bf16[16,16,3072]{2,1,0:T(8,128)(2,1)S(1)} %all-to-all-done.2) | copy-start | bytes 4718596
  218.6 48.6 %all-to-all-start.3 = ((bf16[16,32,3072]{2,1,0:T(8,128)(2,1)}), bf16[16,32,3072]{2,1,0:T(8,128)(2,1)S(1)}, u32[]{:S(2)}, u32[]{:S(2)}) async-start(bf16[16,32,3072]{2,1,0:T(8,128)(2,1)} %bitcast.90), calls=%async_computation.5 | async-start | bytes 6291456 | tf_op jit(solution)/shard_map/all_to_all | solution.py:391
  267.1 1.4 copy-start.6
  270.1 0.9 copy-start.8
  271.0 30.6 %all-to-all-start.4 = ((bf16[16,64,384]{2,1,0:T(8,128)(2,1)}), bf16[16,64,384]{2,1,0:T(8,128)(2,1)S(1)}, u32[]{:S(2)}, u32[]{:S(2)}) async-start(bf16[16,64,384]{2,1,0:T(8,128)(2,1)} %bitcast.85), calls=%async_computation.6 | async-start | bytes 1572864 | tf_op jit(solution)/shard_map/all_to_all | solution.py:444
  280.1 7.0 %copy-start.7 = (bf16[2688,1024]{1,0:T(8,128)(2,1)S(1)}, bf16[2688,1024]{1,0:T(8,128)(2,1)}, u32[]{:S(2)}) copy-start(bf16[2688,1024]{1,0:T(8,128)(2,1)} %all-gather.4.cloned.1.call-done.packed_ref) | copy-start | bytes 16515076
  287.2 2.0 copy-start.4
  289.2 13.2 %copy-start.1 = (bf16[128,384]{1,0:T(8,128)(2,1)S(1)}, bf16[128,384]{1,0:T(8,128)(2,1)}, u32[]{:S(2)}) copy-start(bf16[128,384]{1,0:T(8,128)(2,1)} %param.10) | copy-start | bytes 294916
Sparse Core Ops, SparseCore 0:
  9.8 50.5 all-gather.5
  63.6 91.2 reduce-scatter.4
  163.0 44.7 reduce-scatter.2
  213.4 66.6 all-gather.3
